TPU v7x, 32 devices: a whole 2x2x4 slice. The times are simulated.
32 devices in a mesh: groups: 2 (over x), dp: 2 (over core), tensor: 8 (over z, y).
Axes of the slice: x: 2, y: 2, z: 4, core: 2. Of those that a mesh axis runs over, the one named last changes fastest.
Arguments:
- hidden: bfloat16 [4096, 5120], P(('groups', 'dp')), parts along dimension 0, may hold values from -6 to 6
- context: bfloat16 [4096, 5120], P(('groups', 'dp'), 'tensor'), parts along dimension 0, may hold values from -6 to 6
- w_qkv: bfloat16 [5120, 7168], P(None, 'tensor'), may hold values from -0.078125 to 0.078125
- w_out: bfloat16 [5120, 5120], P('tensor'), may hold values from -0.078125 to 0.078125
- a_qkv: bfloat16 [16, 5120, 64], P(('dp', 'tensor')), may hold values from -0.078125 to 0.078125
- b_qkv: bfloat16 [16, 64, 7168], P(('dp', 'tensor')), may hold values from -0.75 to 0.75
- a_out: bfloat16 [16, 5120, 64], P(('dp', 'tensor')), may hold values from -0.078125 to 0.078125
- b_out: bfloat16 [16, 64, 5120], P(('dp', 'tensor')), may hold values from -0.75 to 0.75
- seg_len: int32 [4, 32], P(('groups', 'dp')), parts along dimension 0, may hold values from 1 to 256, 1024 in all within a row
- seg_use: int32 [4, 32], P(('groups', 'dp')), parts along dimension 0, may hold values from 0 to 5
- used_list: int32 [4, 6], P('groups'), parts along dimension 0, may hold values from 0 to 15, as said below
- adapter_slot: int32 [16], replicated, may hold values from 0 to 15, each once
Outputs:
- qkv: bfloat16 [4096, 7168], P(('groups', 'dp'), 'tensor'), parts along dimension 0
- attn_out: bfloat16 [4096, 5120], P(('groups', 'dp'), 'tensor'), parts along dimension 0
There are 2 independent parts, one for each index of `groups`. A program takes and returns all parts, laid end to end along the dimension named above; an argument that names none is the same for every part. Nothing has to cross between parts.
Inputs may be any that keep to these rules, and one draw needn't show every extreme that they name: `used_list`: each row holds 6 different adapter ids.
All inputs are finite; a program needn't handle non-finite values.
Results may differ from a plain program's by a relative error of at most 0.007.
Values may be sent and summed in bfloat16 or wider, within the bound.
A program may use at most 192 MiB of HBM per device.

v0:
```python
import jax
import jax.numpy as jnp
from jax import lax
from jax.sharding import PartitionSpec as P


def for_sending(value):

    def short(part):
        return part.astype(jnp.bfloat16) if part.dtype == jnp.float32 else part

    return jax.tree.map(short, value)


def shards(
    hidden,
    context,
    w_qkv,
    w_out,
    a_qkv,
    b_qkv,
    a_out,
    b_out,
    seg_len,
    seg_use,
    used_list,
    adapter_slot,
):
    tensor_size = lax.axis_size("tensor")
    dp_size = lax.axis_size("dp")
    tensor_rank = lax.axis_index("tensor")
    dp_rank = lax.axis_index("dp")
    tok_rows, model_width = hidden.shape
    owned_rows = a_qkv.shape[0]
    rank_dim = a_qkv.shape[2]
    joined_cols = b_qkv.shape[2]
    row_part = model_width // tensor_size
    col_part = joined_cols // tensor_size

    def split_rows(weights):
        shaped = weights.reshape(owned_rows, tensor_size, row_part, rank_dim)
        return jnp.transpose(shaped, (1, 0, 2, 3))

    def split_cols(weights, part_width):
        shaped = weights.reshape(owned_rows, rank_dim, tensor_size, part_width)
        return jnp.transpose(shaped, (2, 0, 1, 3))

    pieces = (
        split_rows(a_qkv),
        split_cols(b_qkv, col_part),
        split_rows(a_out),
        split_cols(b_out, row_part),
    )
    my_rows = adapter_slot[used_list[dp_rank]]
    outgoing = tuple(
        (
            jnp.broadcast_to(member[None], (dp_size,) + member.shape).reshape(
                (dp_size * tensor_size,) + member.shape[1:]
            )
            for member in pieces
        )
    )
    received = jax.tree.map(
        lambda part, own: part.astype(own.dtype),
        lax.all_to_all(
            for_sending(outgoing), ("dp", "tensor"), split_axis=0, concat_axis=0, tiled=True
        ),
        outgoing,
    )
    chosen = tuple(
        (jnp.take(member.reshape((-1,) + member.shape[2:]), my_rows, axis=0) for member in received)
    )
    down_qkv, up_qkv, down_out, up_out = chosen
    used_count = my_rows.shape[0]
    seg_ends = jnp.cumsum(seg_len[0])
    positions = jnp.arange(tok_rows, dtype=jnp.int32)
    segment = jnp.sum((positions[:, None] >= seg_ends[None, :]).astype(jnp.int32), axis=1)
    seg_count = seg_len.shape[1]
    slot_tok = jnp.sum(
        jnp.where(
            segment[:, None] == jnp.arange(seg_count, dtype=jnp.int32)[None, :],
            seg_use[0][None, :],
            0,
        ),
        axis=1,
    )
    token_mask = slot_tok[:, None] == jnp.arange(used_count, dtype=jnp.int32)[None, :]
    mask_float = token_mask.astype(jnp.float32)

    def shrink(inputs, down_maps):
        stacked = jnp.transpose(down_maps, (1, 0, 2)).reshape(row_part, used_count * rank_dim)
        products = jnp.dot(inputs, stacked, preferred_element_type=jnp.float32)
        products = products.reshape(tok_rows, used_count, rank_dim)
        return jnp.sum(products * mask_float[:, :, None], axis=1)

    def expand(low_rank, up_maps):
        rounded = low_rank.astype(jnp.bfloat16)
        spread = jnp.where(token_mask[:, :, None], rounded[:, None, :], jnp.zeros((), jnp.bfloat16))
        spread = spread.reshape(tok_rows, used_count * rank_dim)
        stacked = up_maps.reshape(used_count * rank_dim, up_maps.shape[2])
        return jnp.dot(spread, stacked, preferred_element_type=jnp.float32)

    hidden_part = lax.dynamic_slice_in_dim(hidden, tensor_rank * row_part, row_part, 1)
    low_qkv, low_out = lax.psum(
        (shrink(hidden_part, down_qkv), shrink(context, down_out)), "tensor"
    )
    base_qkv = jnp.dot(hidden, w_qkv, preferred_element_type=jnp.float32)
    qkv = (base_qkv + expand(low_qkv, up_qkv)).astype(jnp.bfloat16)
    partial_out = jnp.dot(context, w_out, preferred_element_type=jnp.float32)
    base_out = lax.psum_scatter(partial_out, "tensor", scatter_dimension=1, tiled=True)
    attn_out = (base_out + expand(low_out, up_out)).astype(jnp.bfloat16)
    return (qkv, attn_out)


def solution(mesh):
    placed = (
        P(("groups", "dp"), None),
        P(("groups", "dp"), "tensor"),
        P(None, "tensor"),
        P("tensor", None),
        P(("dp", "tensor"), None, None),
        P(("dp", "tensor"), None, None),
        P(("dp", "tensor"), None, None),
        P(("dp", "tensor"), None, None),
        P(("groups", "dp"), None),
        P(("groups", "dp"), None),
        P("groups", None),
        P(),
    )
    return jax.shard_map(
        shards,
        mesh=mesh,
        in_specs=placed,
        out_specs=(P(("groups", "dp"), "tensor"), P(("groups", "dp"), "tensor")),
        check_vma=False,
    )
```

profile of v0, /device:TPU:0, one launch (start us, length us, event | category | flops | bytes accessed | tf_op | source)
XLA Modules:
  0.0 521.4 jit_solution(16893287104587150136)
XLA Ops:
  7.2 1.3 copy-done
  8.5 14.4 %fusion.32 = f32[1024,5120]{1,0:T(8,128)} fusion(bf16[1024,640]{1,0:T(8,128)(2,1)S(1)} %copy-done, bf16[640,5120]{1,0:T(8,128)(2,1)} %param.17), kind=kOutput, calls=%fused_computation.56 | convolution fusion | flops 6710886400 | bytes 28835840 | tf_op jit(solution)/shard_map/dot_general | solution.py:109
  22.9 1.1 copy-done.3
  24.1 1.2 broadcast_in_dim.128
  25.3 7.4 %all-to-all-start = ((bf16[16,1,640,64]{2,3,1,0:T(8,128)(2,1)}), bf16[16,1,640,64]{2,3,1,0:T(8,128)(2,1)S(1)}, u32[]{:S(2)}, u32[]{:S(2)}) async-start(bf16[16,1,640,64]{2,3,1,0:T(8,128)(2,1)} %bitcast.5), calls=%async_computation | async-start | bytes 2621440 | tf_op jit(solution)/shard_map/all_to_all | solution.py:65
  32.9 60.8 %all-to-all-done = bf16[16,1,640,64]{2,3,1,0:T(8,128)(2,1)S(1)} async-done(((bf16[16,1,640,64]{2,3,1,0:T(8,128)(2,1)}), bf16[16,1,640,64]{2,3,1,0:T(8,128)(2,1)S(1)}, u32[]{:S(2)}, u32[]{:S(2)}) %all-to-all-start) | async-done | bytes 1310752 | tf_op jit(solution)/shard_map/all_to_all | solution.py:65
  93.7 1.2 broadcast_in_dim.138
  94.9 7.3 %all-to-all-start.2 = ((bf16[16,1,640,64]{2,3,1,0:T(8,128)(2,1)}), bf16[16,1,640,64]{2,3,1,0:T(8,128)(2,1)}, u32[]{:S(2)}, u32[]{:S(2)}) async-start(bf16[16,1,640,64]{2,3,1,0:T(8,128)(2,1)} %bitcast.18), calls=%async_computation.3 | async-start | bytes 2621440 | tf_op jit(solution)/shard_map/all_to_all | solution.py:65
  102.5 58.0 %all-to-all-done.2 = bf16[16,1,640,64]{2,3,1,0:T(8,128)(2,1)} async-done(((bf16[16,1,640,64]{2,3,1,0:T(8,128)(2,1)}), bf16[16,1,640,64]{2,3,1,0:T(8,128)(2,1)}, u32[]{:S(2)}, u32[]{:S(2)}) %all-to-all-start.2) | async-done | bytes 1310752 | tf_op jit(solution)/shard_map/all_to_all | solution.py:65
  160.5 1.2 broadcast_in_dim.143
  161.8 8.7 %all-to-all-start.3 = ((bf16[16,1,64,640]{3,2,1,0:T(8,128)(2,1)}), bf16[16,1,64,640]{3,2,1,0:T(8,128)(2,1)}, u32[]{:S(2)}, u32[]{:S(2)}) async-start(bf16[16,1,64,640]{3,2,1,0:T(8,128)(2,1)} %bitcast.26), calls=%async_computation.4 | async-start | bytes 2621440 | tf_op jit(solution)/shard_map/all_to_all | solution.py:65
  170.4 0.7 copy.34
  171.1 0.8 reduce-window.8
  171.9 0.6 reduce
  173.4 1.1 gather_fusion
  174.5 0.6 compare_select_fusion
  175.3 0.6 compare_and_fusion
  175.9 0.6 fusion.23
  176.5 52.2 %all-to-all-done.3 = bf16[16,1,64,640]{3,2,1,0:T(8,128)(2,1)} async-done(((bf16[16,1,64,640]{3,2,1,0:T(8,128)(2,1)}), bf16[16,1,64,640]{3,2,1,0:T(8,128)(2,1)}, u32[]{:S(2)}, u32[]{:S(2)}) %all-to-all-start.3) | async-done | bytes 1310752 | tf_op jit(solution)/shard_map/all_to_all | solution.py:65
  228.7 1.5 broadcast_in_dim.134
  230.2 8.7 %all-to-all-start.1 = ((bf16[16,1,64,896]{3,2,1,0:T(8,128)(2,1)}), bf16[16,1,64,896]{3,2,1,0:T(8,128)(2,1)}, u32[]{:S(2)}, u32[]{:S(2)}) async-start(bf16[16,1,64,896]{3,2,1,0:T(8,128)(2,1)} %bitcast.13), calls=%async_computation.1 | async-start | bytes 3670016 | tf_op jit(solution)/shard_map/all_to_all | solution.py:65
  239.0 16.9 %fusion.31 = f32[1024,896]{1,0:T(8,128)} fusion(bf16[1024,5120]{1,0:T(8,128)(2,1)} %param.14, bf16[5120,896]{1,0:T(8,128)(2,1)} %param.16), kind=kOutput, calls=%fused_computation.55 | convolution fusion | flops 9395240960 | bytes 23330816 | tf_op jit(solution)/shard_map/dot_general | solution.py:107
  255.8 0.6 gather_fusion.3
  256.5 2.2 multiply_reduce_fusion.1
  258.7 2.0 gather_fusion.4
  260.7 0.8 fusion.33
  261.7 2.0 gather_fusion.2
  263.7 96.3 %all-reduce.2 = (bf16[1024,64]{0,1:T(8,128)(2,1)S(1)}, bf16[1024,64]{0,1:T(8,128)(2,1)S(1)}) all-reduce(f32[1024,64]{0,1:T(8,128)S(1)} %multiply_reduce_fusion.1, f32[1024,64]{0,1:T(8,128)S(1)} %multiply_reduce_fusion), channel_id=1, replica_groups=mesh['groups'=2,'dp'=2,'tensor'=8] {'tensor'}, use_global_device_ids=true, to_apply=%region_4.6 | all-reduce | flops 131072 | bytes 786432 | tf_op jit(solution)/shard_map/psum | solution.py:104
  360.1 2.3 gather_fusion.1
  362.3 4.6 fusion
  366.9 143.9 %reduce-scatter.2.cloned.1.call-done = f32[1024,640]{1,0:T(8,128)} async-done(((f32[1024,5120]{1,0:T(8,128)}), f32[1024,640]{1,0:T(8,128)}) %reduce-scatter.2.cloned.1.call-update) | async-done | bytes 2621456 | tf_op jit(solution)/shard_map/reduce_scatter | solution.py:110
  510.8 3.8 fusion.1
  (40 shorter events, 1.9 us)
Async XLA Ops:
  7.2 1.3 copy-start
  7.2 503.6 %reduce-scatter.2.cloned.1.call-start = ((), (), s32[]{:S(2)}) async-start(), calls=%async_computation.5 | async-start | bytes 23592960 | tf_op jit(solution)/shard_map/reduce_scatter | solution.py:110
  22.8 1.1 copy-start.3
  24.1 8.6 %copy-start.4 = (bf16[1,5120,64]{1,2,0:T(8,128)(2,1)S(1)}, bf16[1,5120,64]{1,2,0:T(8,128)(2,1)}, u32[]{:S(2)}) copy-start(bf16[1,5120,64]{1,2,0:T(8,128)(2,1)} %param.20) | copy-start | bytes 1966084
  25.3 68.4 %all-to-all-start = ((bf16[16,1,640,64]{2,3,1,0:T(8,128)(2,1)}), bf16[16,1,640,64]{2,3,1,0:T(8,128)(2,1)S(1)}, u32[]{:S(2)}, u32[]{:S(2)}) async-start(bf16[16,1,640,64]{2,3,1,0:T(8,128)(2,1)} %bitcast.5), calls=%async_computation | async-start | bytes 2621440 | tf_op jit(solution)/shard_map/all_to_all | solution.py:65
  94.9 7.3 %copy-start.5 = (bf16[1,64,5120]{2,1,0:T(8,128)(2,1)S(1)}, bf16[1,64,5120]{2,1,0:T(8,128)(2,1)}, u32[]{:S(2)}) copy-start(bf16[1,64,5120]{2,1,0:T(8,128)(2,1)} %param.21) | copy-start | bytes 1966084
  94.9 65.6 %all-to-all-start.2 = ((bf16[16,1,640,64]{2,3,1,0:T(8,128)(2,1)}), bf16[16,1,640,64]{2,3,1,0:T(8,128)(2,1)}, u32[]{:S(2)}, u32[]{:S(2)}) async-start(bf16[16,1,640,64]{2,3,1,0:T(8,128)(2,1)} %bitcast.18), calls=%async_computation.3 | async-start | bytes 2621440 | tf_op jit(solution)/shard_map/all_to_all | solution.py:65
  102.5 67.9 %copy-start.7 = (s32[1,32]{1,0:T(1,128)S(1)}, s32[1,32]{1,0:T(1,128)}, u32[]{:S(2)}) copy-start(s32[1,32]{1,0:T(1,128)} %param.22) | copy-start | bytes 388
  161.8 10.8 %copy-start.2 = (bf16[1,64,7168]{2,1,0:T(8,128)(2,1)S(1)}, bf16[1,64,7168]{2,1,0:T(8,128)(2,1)}, u32[]{:S(2)}) copy-start(bf16[1,64,7168]{2,1,0:T(8,128)(2,1)} %param.19) | copy-start | bytes 2752516
  161.8 66.9 %all-to-all-start.3 = ((bf16[16,1,64,640]{3,2,1,0:T(8,128)(2,1)}), bf16[16,1,64,640]{3,2,1,0:T(8,128)(2,1)}, u32[]{:S(2)}, u32[]{:S(2)}) async-start(bf16[16,1,64,640]{3,2,1,0:T(8,128)(2,1)} %bitcast.26), calls=%async_computation.4 | async-start | bytes 2621440 | tf_op jit(solution)/shard_map/all_to_all | solution.py:65
  172.7 0.7 copy-start.9
  172.7 0.7 copy-start.1
  172.7 2.4 copy-start.6
  172.7 2.5 copy-start.8
  230.2 129.8 %all-to-all-start.1 = ((bf16[16,1,64,896]{3,2,1,0:T(8,128)(2,1)}), bf16[16,1,64,896]{3,2,1,0:T(8,128)(2,1)}, u32[]{:S(2)}, u32[]{:S(2)}) async-start(bf16[16,1,64,896]{3,2,1,0:T(8,128)(2,1)} %bitcast.13), calls=%async_computation.1 | async-start | bytes 3670016 | tf_op jit(solution)/shard_map/all_to_all | solution.py:65
Sparse Core Ops, SparseCore 0:
  23.0 487.7 reduce-scatter.1
where the time goes:
time: 522 us; the launch traced here: 521 us
  waiting for transfers between devices  315 us (60%)
  blocking collectives  96.3 us (18%)
  matrix products  42.5 us (8%)
  starting transfers between devices  32.1 us (6%)
  local copies, waits for them, and re-layouts  17.4 us (3%)
  between operations  14.4 us (3%)
    all_to_all x4, waiting for transfers between devices, shards(): lax.all_to_all(for_sending(outgoing), ('dp', 'tensor'), split_axis=0, con...  171 us
    reduce_scatter x1, waiting for transfers between devices, shards(): lax.psum_scatter(partial_out, 'tensor', scatter_dimension=1, tiled=True)  144 us
    psum x1, blocking collectives, shards(): lax.psum((shrink(hidden_part, down_qkv), shrink(context, down_out)), 'ten...  96.3 us
    all_to_all x4, starting transfers between devices, shards(): lax.all_to_all(for_sending(outgoing), ('dp', 'tensor'), split_axis=0, con...  32.1 us
    dot_general x1, matrix products, shards(): base_qkv = jnp.dot(hidden, w_qkv, preferred_element_type=jnp.float32)  16.9 us
    dot_general x1, matrix products, shards(): partial_out = jnp.dot(context, w_out, preferred_element_type=jnp.float32)  14.4 us
  transfers between devices with their start and end apart: 5, of which 4 were waited for; matrix products, arithmetic and copies ran while one was open for 8% of the time, Pallas kernels for 0%

commit v1 on v0

v1 whole, which is shorter than its diff:
```python
import jax
import jax.numpy as jnp
from jax import lax
from jax.sharding import PartitionSpec as P


def chunk_order(depth):
    rows = []
    for z in range(depth):
        row = []
        for s in range(depth - 1):
            for d, ok in ((z + depth - 1 - s, s >= z), (z - depth + 1 + s, s >= depth - 1 - z)):
                if ok:
                    row.append(d)
        rows.append(row + [z])
    return rows


def token_rows(seg_len, seg_use, row_of_use, tok_rows):
    count = seg_len.shape[0]
    order = jnp.arange(count, dtype=jnp.int32)
    ends = jnp.sum(jnp.where(order[None, :] <= order[:, None], seg_len[None, :], 0), axis=1)
    used = jnp.arange(row_of_use.shape[0], dtype=jnp.int32)
    seg_row = jnp.sum(jnp.where(seg_use[:, None] == used[None, :], row_of_use[None, :], 0), axis=1)
    positions = jnp.arange(tok_rows, dtype=jnp.int32)
    inside = (positions[:, None] >= (ends - seg_len)[None, :]) & (positions[:, None] < ends[None, :])
    return jnp.sum(jnp.where(inside, seg_row[None, :], 0), axis=1)


def shards(
    hidden,
    context,
    w_qkv,
    w_out,
    a_qkv,
    b_qkv,
    a_out,
    b_out,
    seg_len,
    seg_use,
    used_list,
    adapter_slot,
):
    f32, bf16 = jnp.float32, jnp.bfloat16
    tensor_size = lax.axis_size("tensor")
    dp_size = lax.axis_size("dp")
    t = lax.axis_index("tensor")
    dp_rank = lax.axis_index("dp")
    tok_rows, model_width = hidden.shape
    owned, _, rank = a_qkv.shape
    out_part = model_width // tensor_size
    qkv_part = b_qkv.shape[2] // tensor_size
    depth = tensor_size // 2
    z, y = t // 2, t % 2

    used = used_list[dp_rank][:, None] == jnp.arange(adapter_slot.shape[0], dtype=jnp.int32)[None, :]
    row_of_use = jnp.sum(jnp.where(used, adapter_slot[None, :], 0), axis=1)
    store_row = token_rows(seg_len[0], seg_use[0], row_of_use, tok_rows)

    def out_cols(d, side):
        return lax.dynamic_slice_in_dim(w_out, (2 * d + side) * out_part, out_part, 1)

    def partial(d, side):
        return jnp.dot(context, out_cols(d, side), preferred_element_type=f32)

    order = jnp.asarray(chunk_order(depth), jnp.int32)[z]
    swap = [(i, i ^ 1) for i in range(tensor_size)]
    both = [(0, 1), (1, 0)]

    def split(maps, part):
        return jnp.transpose(maps.reshape(owned, rank, tensor_size, part), (2, 0, 1, 3))

    a_out_t = jnp.transpose(a_out, (0, 2, 1))
    sent = jnp.concatenate(
        (split(a_out_t, out_part), split(b_out, out_part), split(b_qkv, qkv_part)), axis=3
    )

    reduced, up, down = [], None, None

    def chosen(d):
        value = reduced[0]
        for k in range(1, len(reduced)):
            value = jnp.where(order[k] == d, reduced[k], value)
        return value

    for k in range(depth):
        mine = lax.ppermute(partial(order[k], 1 - y).astype(bf16), "tensor", swap)
        reduced.append(mine.astype(f32) + partial(order[k], y))
        if k < depth - 1:
            s = k
            outgoing_up = chosen(z + depth - 1 - s)
            outgoing_down = chosen(z - depth + 1 + s)
            if s > 0:
                outgoing_up = outgoing_up + up.astype(f32)
                outgoing_down = outgoing_down + down.astype(f32)
            up_pairs = [(2 * i + j, 2 * i + 2 + j) for i in range(s + 1) for j in range(2)]
            down_pairs = [
                (2 * i + j, 2 * i - 2 + j) for i in range(depth - 1 - s, depth) for j in range(2)
            ]
            up = lax.ppermute(outgoing_up.astype(bf16), "tensor", up_pairs)
            down = lax.ppermute(outgoing_down.astype(bf16), "tensor", down_pairs)
        if k == 0:
            got = lax.all_to_all(sent, "tensor", split_axis=0, concat_axis=0, tiled=True)
            got = got.reshape((tensor_size * owned,) + got.shape[2:])
            other = lax.ppermute(got, "dp", both)
            a_other = lax.ppermute(a_qkv, "dp", both)
    base_out = reduced[-1] + up.astype(f32) + down.astype(f32)

    half = tensor_size * owned
    first = dp_rank * half
    second = (1 - dp_rank) * half
    rows = jnp.arange(half, dtype=jnp.int32)
    row_ids = jnp.concatenate((first + rows, second + rows))
    maps = jnp.concatenate((got, other), axis=0)
    down_out = maps[:, :, :out_part]
    up_out = maps[:, :, out_part : 2 * out_part].reshape(-1, out_part)
    up_qkv = maps[:, :, 2 * out_part :].reshape(-1, qkv_part)
    row_mask = store_row[:, None] == row_ids[None, :]

    own = jnp.arange(owned, dtype=jnp.int32) + t * owned
    own_ids = jnp.concatenate((first + own, second + own))
    own_mask = store_row[:, None] == own_ids[None, :]

    def pick(products, mask):
        shaped = products.reshape(tok_rows, mask.shape[1], rank)
        return jnp.sum(jnp.where(mask[:, :, None], shaped, 0.0), axis=1)

    a_two = jnp.concatenate((a_qkv, a_other), axis=0)
    low_a = jnp.einsum("td,rdk->trk", hidden, a_two, preferred_element_type=f32)
    low_b = jnp.einsum("td,rkd->trk", context, down_out, preferred_element_type=f32)
    low_qkv, low_out = lax.psum((pick(low_a, own_mask), pick(low_b, row_mask)), "tensor")

    def expand(low, up_maps):
        spread = jnp.where(row_mask[:, :, None], low.astype(bf16)[:, None, :], jnp.zeros((), bf16))
        return jnp.dot(spread.reshape(tok_rows, -1), up_maps, preferred_element_type=f32)

    base_qkv = jnp.dot(hidden, w_qkv, preferred_element_type=f32)
    qkv = (base_qkv + expand(low_qkv, up_qkv)).astype(bf16)
    attn_out = (base_out + expand(low_out, up_out)).astype(bf16)
    return (qkv, attn_out)


def solution(mesh):
    placed = (
        P(("groups", "dp"), None),
        P(("groups", "dp"), "tensor"),
        P(None, "tensor"),
        P("tensor", None),
        P(("dp", "tensor"), None, None),
        P(("dp", "tensor"), None, None),
        P(("dp", "tensor"), None, None),
        P(("dp", "tensor"), None, None),
        P(("groups", "dp"), None),
        P(("groups", "dp"), None),
        P("groups", None),
        P(),
    )
    return jax.shard_map(
        shards,
        mesh=mesh,
        in_specs=placed,
        out_specs=(P(("groups", "dp"), "tensor"), P(("groups", "dp"), "tensor")),
        check_vma=False,
    )
```

time: 522 us -> 225 us (0.43)
  waiting for transfers between devices: 315 us -> 41.6 us
  blocking collectives: 96.3 us -> 52.7 us
  matrix products: 42.5 us -> 70.3 us
  other arithmetic: 3.65 us -> 15.7 us
  local copies, waits for them, and re-layouts: 17.4 us -> 6.14 us
  between operations: 14.4 us -> 7.32 us
    all_to_all x4 -> x1, waiting for transfers between devices: 171 us -> 10.3 us  [shards(): lax.all_to_all(sent, 'tensor', split_axis=0, concat_axis=0, tiled=True)]
    reduce_scatter x1 -> x0, waiting for transfers between devices: 144 us -> none  [shards(): lax.psum_scatter(partial_out, 'tensor', scatter_dimension=1, tiled=True)]
    psum x1, blocking collectives: 96.3 us -> 52.7 us  [shards(): lax.psum((pick(low_a, own_mask), pick(low_b, row_mask)), 'tensor')]
    ppermute x0 -> x12, waiting for transfers between devices: none -> 31.3 us  [the longest x4 27.6 us: shards(): mine = lax.ppermute(partial(order[k], 1 - y).astype(bf16), 'tensor', swap)]
    dot_general x6 -> x13, matrix products: 42.5 us -> 70.3 us  [the longest x8 29.2 us: partial(): return jnp.dot(context, out_cols(d, side), preferred_element_type=f32)]
    all_to_all x4 -> x1, starting transfers between devices: 32.1 us -> 5.29 us  [shards(): lax.all_to_all(sent, 'tensor', split_axis=0, concat_axis=0, tiled=True)]
    ppermute x0 -> x12, starting transfers between devices: none -> 25.3 us  [the longest x3 13.7 us: shards(): up = lax.ppermute(outgoing_up.astype(bf16), 'tensor', up_pairs)]
    convert_element_type x1 -> x2, other arithmetic: 0.01 us -> 11.6 us  [shards(): up = lax.ppermute(outgoing_up.astype(bf16), 'tensor', up_pairs)]
  transfers between devices with their start and end apart: 5 -> 13, of which waited for: 4 -> 4; matrix products, arithmetic and copies ran while one was open for 8% -> 32% of each run, Pallas kernels for 0% -> 0%
where the time goes in v1:
time: 225 us; the launch traced here: 224 us
  matrix products  70.3 us (31%)
  blocking collectives  52.7 us (23%)
  waiting for transfers between devices  41.6 us (18%)
  starting transfers between devices  30.6 us (14%)
  other arithmetic  15.7 us (7%)
  between operations  7.32 us (3%)
  local copies, waits for them, and re-layouts  6.14 us (3%)
    psum x1, blocking collectives, shards(): lax.psum((pick(low_a, own_mask), pick(low_b, row_mask)), 'tensor')  52.7 us
    dot_general x8, matrix products, partial(): return jnp.dot(context, out_cols(d, side), preferred_element_type=f32)  29.2 us
    ppermute x4, waiting for transfers between devices, shards(): mine = lax.ppermute(partial(order[k], 1 - y).astype(bf16), 'tensor', swap)  27.6 us
    dot_general x1, matrix products, shards(): base_qkv = jnp.dot(hidden, w_qkv, preferred_element_type=f32)  16.8 us
    ppermute x3, starting transfers between devices, shards(): up = lax.ppermute(outgoing_up.astype(bf16), 'tensor', up_pairs)  13.7 us
    dot_general x2, matrix products, expand(): jnp.dot(spread.reshape(tok_rows, -1), up_maps, preferred_element_type=f32)  12.1 us
    convert_element_type x2, other arithmetic, shards(): up = lax.ppermute(outgoing_up.astype(bf16), 'tensor', up_pairs)  11.6 us
    all_to_all x1, waiting for transfers between devices, shards(): lax.all_to_all(sent, 'tensor', split_axis=0, concat_axis=0, tiled=True)  10.3 us
  transfers between devices with their start and end apart: 13, of which 4 were waited for; matrix products, arithmetic and copies ran while one was open for 32% of the time, Pallas kernels for 0%

profile of v1, /device:TPU:0, one launch (start us, length us, event | category | flops | bytes accessed | tf_op | source)
XLA Modules:
  0.0 224.4 jit_solution(10064359043227784959)
XLA Ops:
  2.8 3.4 %fusion.22 = bf16[1024,640]{0,1:T(8,128)(2,1)} fusion(bf16[1024,640]{1,0:T(8,128)(2,1)S(1)} %copy-done, bf16[640,5120]{1,0:T(8,128)(2,1)} %param.16, s32[]{:T(128)S(6)} %select_n.128), kind=kOutput, calls=%fused_computation.37 | convolution fusion | flops 839516160 | bytes 3440644 | tf_op jit(solution)/shard_map/dot_general | solution.py:64
  6.2 3.0 %collective-permute-start.5 = (bf16[1024,640]{0,1:T(8,128)(2,1)}, bf16[1024,640]{0,1:T(8,128)(2,1)}, u32[]{:S(2)}, u32[]{:S(2)}) collective-permute-start(bf16[1024,640]{0,1:T(8,128)(2,1)} %fusion.22), channel_id=1, source_target_pairs={{0,1},{1,0},{2,3},{3,2},{4,5},{5,4},{6,7},{7,6},{8,9},{9,8},{10,11... | collective-permute-start | bytes 3932168 | tf_op jit(solution)/shard_map/ppermute | solution.py:87
  9.8 3.4 %fusion.21 = bf16[1024,640]{0,1:T(8,128)(2,1)} fusion(bf16[1024,640]{1,0:T(8,128)(2,1)S(1)} %copy-done, bf16[640,5120]{1,0:T(8,128)(2,1)} %param.16, s32[]{:T(128)S(6)} %select_n.126), kind=kOutput, calls=%fused_computation.36 | convolution fusion | flops 839516160 | bytes 3440644 | tf_op jit(solution)/shard_map/dot_general | solution.py:64
  14.0 3.6 %fusion.20 = bf16[1024,640]{0,1:T(8,128)(2,1)} fusion(bf16[1024,640]{1,0:T(8,128)(2,1)S(1)} %copy-done, bf16[640,5120]{1,0:T(8,128)(2,1)} %param.16, s32[]{:T(128)S(6)} %select_n.123), kind=kOutput, calls=%fused_computation.35 | convolution fusion | flops 839516160 | bytes 3440644 | tf_op jit(solution)/shard_map/dot_general | solution.py:64
  17.6 2.0 collective-permute-start.3
  20.3 1.7 copy.25
  22.0 5.3 %all-to-all-start = ((bf16[8,1,64,2176]{3,2,1,0:T(8,128)(2,1)}), bf16[8,1,64,2176]{3,2,1,0:T(8,128)(2,1)S(1)}, u32[]{:S(2)}, u32[]{:S(2)}) async-start(bf16[8,1,64,2176]{3,2,1,0:T(8,128)(2,1)} %copy.25), calls=%async_computation | async-start | bytes 4456448 | tf_op jit(solution)/shard_map/all_to_all | solution.py:103
  27.3 16.8 %fusion.80 = f32[1024,896]{1,0:T(8,128)} fusion(bf16[1024,5120]{1,0:T(8,128)(2,1)} %param.13, bf16[5120,896]{1,0:T(8,128)(2,1)} %param.15), kind=kOutput, calls=%fused_computation.102 | convolution fusion | flops 9395240960 | bytes 23330816 | tf_op jit(solution)/shard_map/dot_general | solution.py:137
  44.2 8.0 %collective-permute-done.5 = bf16[1024,640]{0,1:T(8,128)(2,1)} collective-permute-done((bf16[1024,640]{0,1:T(8,128)(2,1)}, bf16[1024,640]{0,1:T(8,128)(2,1)}, u32[]{:S(2)}, u32[]{:S(2)}) %collective-permute-start.5) | collective-permute-done | bytes 1310752 | tf_op jit(solution)/shard_map/ppermute | solution.py:87
  52.2 4.7 %fusion.79 = (bf16[1024,640]{0,1:T(8,128)(2,1)}, f32[1024,640]{0,1:T(8,128)}) fusion(bf16[1024,640]{1,0:T(8,128)(2,1)S(1)} %copy-done, bf16[640,5120]{1,0:T(8,128)(2,1)} %param.16, s32[]{:T(128)S(6)} %select_n.129, bf16[1024,640]{0,1:T(8,128)(2,1)} %collective-permute-done.5), kind=kOutput, calls=%fused_computation.101 | convolution fusion | flops 840826880 | bytes 7372804 | tf_op jit(solution)/shard_map/dot_general | solution.py:64
  56.9 3.0 %collective-permute-start.6 = (bf16[1024,640]{0,1:T(8,128)(2,1)}, bf16[1024,640]{0,1:T(8,128)(2,1)}, u32[]{:S(2)}, u32[]{:S(2)}) collective-permute-start(bf16[1024,640]{0,1:T(8,128)(2,1)} %get-tuple-element.20), channel_id=1, source_target_pairs={{0,2},{1,3},{8,10},{9,11},{16,18},{17,19},{24,26},{25,27}} | collective-permute-start | bytes 3932168 | tf_op jit(solution)/shard_map/ppermute | solution.py:100
  59.9 1.8 collective-permute-start.9
  65.5 19.6 %collective-permute-done.4 = bf16[1024,640]{0,1:T(8,128)(2,1)} collective-permute-done((bf16[1024,640]{0,1:T(8,128)(2,1)}, bf16[1024,640]{0,1:T(8,128)(2,1)}, u32[]{:S(2)}, u32[]{:S(2)}) %collective-permute-start.4) | collective-permute-done | bytes 1310752 | tf_op jit(solution)/shard_map/ppermute | solution.py:87
  85.1 2.8 %bitcast_add_fusion.3 = f32[1024,640]{0,1:T(8,128)S(1)} fusion(bf16[1024,640]{0,1:T(8,128)(2,1)} %collective-permute-done.4, bf16[1024,640]{1,0:T(8,128)(2,1)S(1)} %copy-done, bf16[640,5120]{1,0:T(8,128)(2,1)} %param.16, s32[]{:T(128)S(6)} %select_n.127), kind=kOutput, calls=%fused_computation.13 | convolution fusion | flops 840171520 | bytes 6062084 | tf_op jit(solution)/shard_map/dot_general | solution.py:64
  87.9 3.6 %collective-permute-done.6 = bf16[1024,640]{0,1:T(8,128)(2,1)} collective-permute-done((bf16[1024,640]{0,1:T(8,128)(2,1)}, bf16[1024,640]{0,1:T(8,128)(2,1)}, u32[]{:S(2)}, u32[]{:S(2)}) %collective-permute-start.6) | collective-permute-done | bytes 1310752 | tf_op jit(solution)/shard_map/ppermute | solution.py:100
  91.6 4.3 %add_convert_fusion.3 = (bf16[1024,640]{0,1:T(8,128)(2,1)}, bf16[1024,640]{0,1:T(8,128)(2,1)}) fusion(bf16[1024,640]{0,1:T(8,128)(2,1)} %collective-permute-done.6, f32[1024,640]{0,1:T(8,128)S(1)} %bitcast_add_fusion.3, f32[1024,640]{0,1:T(8,128)S(1)} %copy-done.1, pred[]{:T(512)S(6)} %eq.100, bf16[1024,640]{0,1:T(8,128)(2,1)} %collective-permute-done.9, ...), kind=kLoop, calls=%fused_computation.21 | loop fusion | flops 5242880 | bytes 10485762 | tf_op jit(solution)/shard_map/convert_element_type | solution.py:100
  95.9 1.7 collective-permute-start.10
  97.6 5.0 %collective-permute-start.7 = (bf16[1024,640]{0,1:T(8,128)(2,1)}, bf16[1024,640]{0,1:T(8,128)(2,1)}, u32[]{:S(2)}, u32[]{:S(2)}) collective-permute-start(bf16[1024,640]{0,1:T(8,128)(2,1)} %get-tuple-element.14), channel_id=1, source_target_pairs={{0,2},{1,3},{2,4},{3,5},{8,10},{9,11},{10,12},{11,13},{16,18},{17,... | collective-permute-start | bytes 3932168 | tf_op jit(solution)/shard_map/ppermute | solution.py:100
  104.0 3.9 %fusion.55 = f32[640,1024]{1,0:T(8,128)} fusion(bf16[1024,640]{1,0:T(8,128)(2,1)S(1)} %copy-done, bf16[640,5120]{1,0:T(8,128)(2,1)} %param.16, s32[]{:T(128)S(6)} %select_n.124), kind=kOutput, calls=%fused_computation.57 | convolution fusion | flops 838860800 | bytes 4751364 | tf_op jit(solution)/shard_map/dot_general | solution.py:64
  107.9 10.3 %all-to-all-done = bf16[8,1,64,2176]{3,2,1,0:T(8,128)(2,1)S(1)} async-done(((bf16[8,1,64,2176]{3,2,1,0:T(8,128)(2,1)}), bf16[8,1,64,2176]{3,2,1,0:T(8,128)(2,1)S(1)}, u32[]{:S(2)}, u32[]{:S(2)}) %all-to-all-start) | async-done | bytes 2228256 | tf_op jit(solution)/shard_map/all_to_all | solution.py:103
  118.2 3.5 %fusion.19 = bf16[1024,640]{0,1:T(8,128)(2,1)} fusion(bf16[1024,640]{1,0:T(8,128)(2,1)S(1)} %copy-done, bf16[640,5120]{1,0:T(8,128)(2,1)} %param.16, s32[]{:T(128)S(6)} %select_n.120), kind=kOutput, calls=%fused_computation.34 | convolution fusion | flops 839516160 | bytes 3440644 | tf_op jit(solution)/shard_map/dot_general | solution.py:64
  121.7 3.9 %fusion.58 = f32[640,1024]{1,0:T(8,128)} fusion(bf16[1024,640]{1,0:T(8,128)(2,1)S(1)} %copy-done, bf16[640,5120]{1,0:T(8,128)(2,1)} %param.16, s32[]{:T(128)S(6)} %select_n.121), kind=kOutput, calls=%fused_computation.60 | convolution fusion | flops 838860800 | bytes 4751364 | tf_op jit(solution)/shard_map/dot_general | solution.py:64
  128.9 1.8 collective-permute-start.2
  130.7 7.3 %add_convert_fusion.2 = (bf16[1024,640]{0,1:T(8,128)(2,1)}, bf16[1024,640]{0,1:T(8,128)(2,1)}) fusion(bf16[1024,640]{0,1:T(8,128)(2,1)} %collective-permute-done.7, f32[1024,640]{0,1:T(8,128)} %copy-done.2, f32[1024,640]{0,1:T(8,128)} %get-tuple-element.21, f32[640,1024]{1,0:T(8,128)} %fusion.55, bf16[1024,640]{0,1:T(8,128)(2,1)} %collective-permute-done.3, ...), kind=kLoop, calls=%fused_computation.20 | loop fusion | flops 7864320 | bytes 14417924 | tf_op jit(solution)/shard_map/convert_element_type | solution.py:100
  138.0 1.3 collective-permute-start.11
  139.3 5.6 %collective-permute-start.8 = (bf16[1024,640]{0,1:T(8,128)(2,1)}, bf16[1024,640]{0,1:T(8,128)(2,1)}, u32[]{:S(2)}, u32[]{:S(2)}) collective-permute-start(bf16[1024,640]{0,1:T(8,128)(2,1)} %get-tuple-element.12), channel_id=1, source_target_pairs={{0,2},{1,3},{2,4},{3,5},{4,6},{5,7},{8,10},{9,11},{10,12},{11,13},... | collective-permute-start | bytes 3932168 | tf_op jit(solution)/shard_map/ppermute | solution.py:100
  144.9 8.5 %fusion.40 = f32[1024,64]{0,1:T(8,128)} fusion(bf16[1024,5120]{1,0:T(8,128)(2,1)} %param.13, bf16[1,5120,64]{1,2,0:T(8,128)(2,1)} %collective-permute-done, bf16[1,5120,64]{1,2,0:T(8,128)(2,1)S(1)} %copy-done.8, pred[1024,2]{0,1:T(4,128)(4,1)S(1)} %copy-done.7), kind=kOutput, calls=%fused_computation.47 | convolution fusion | flops 1343029248 | bytes 12060672 | tf_op jit(solution)/shard_map/td,rdk->trk/dot_general | solution.py:129
  153.5 3.6 %fusion.2 = f32[1024,64]{0,1:T(8,128)} fusion(pred[1024,16]{0,1:T(8,128)(4,1)S(1)} %copy-done.6, bf16[8,64,2176]{2,1,0:T(8,128)(2,1)S(1)} %bitcast.111, bf16[8,64,2176]{2,1,0:T(8,128)(2,1)} %collective-permute-done.1, bf16[1024,640]{1,0:T(8,128)(2,1)S(1)} %copy-done), kind=kOutput, calls=%fused_computation.7 | convolution fusion | flops 1344864256 | bytes 6045696 | tf_op jit(solution)/shard_map/td,rkd->trk/dot_general | solution.py:130
  157.1 52.7 %all-reduce.2 = (bf16[1024,64]{0,1:T(8,128)(2,1)}, bf16[1024,64]{0,1:T(8,128)(2,1)}) all-reduce(f32[1024,64]{0,1:T(8,128)} %fusion.40, f32[1024,64]{0,1:T(8,128)} %fusion.2), channel_id=1, replica_groups=mesh['groups'=2,'dp'=2,'tensor'=8] {'tensor'}, use_global_device_ids=true, to_apply=%region_5.6 | all-reduce | flops 131072 | bytes 786432 | tf_op jit(solution)/shard_map/psum | solution.py:131
  209.8 6.1 %fusion.4 = bf16[1024,640]{0,1:T(8,128)(2,1)} fusion(f32[640,1024]{1,0:T(8,128)} %fusion.58, bf16[1024,640]{0,1:T(8,128)(2,1)} %collective-permute-done.11, bf16[1024,640]{0,1:T(8,128)(2,1)} %collective-permute-done.8, bf16[1024,640]{0,1:T(8,128)(2,1)} %collective-permute-done.2, bf16[8,64,2176]{2,1,0:T(8,128)(2,1)} %collective-permute-done.1, ...), kind=kOutput, calls=%fused_computation.11 | convolution fusion | flops 1351090176 | bytes 12468224 | tf_op jit(solution)/shard_map/dot_general | solution.py:135
  215.9 2.4 %copy.27 = bf16[1024,640]{1,0:T(8,128)(2,1)} copy(bf16[1024,640]{0,1:T(8,128)(2,1)} %fusion.4) | data formatting | bytes 2621440
  218.4 6.0 %fusion.3 = bf16[1024,896]{1,0:T(8,128)(2,1)} fusion(f32[1024,896]{1,0:T(8,128)} %fusion.80, bf16[8,64,2176]{2,1,0:T(8,128)(2,1)S(1)} %bitcast.113, bf16[8,64,2176]{2,1,0:T(8,128)(2,1)} %collective-permute-done.1, pred[1024,16]{0,1:T(8,128)(4,1)S(1)} %copy-done.6, bf16[1024,64]{0,1:T(8,128)(2,1)} %get-tuple-element.10), kind=kOutput, calls=%fused_computation.9 | convolution fusion | flops 1882849280 | bytes 10108928 | tf_op jit(solution)/shard_map/dot_general | solution.py:135
  (53 shorter events, 6.2 us)
Async XLA Ops:
  0.6 2.2 copy-start
  6.2 45.9 %collective-permute-start.5 = (bf16[1024,640]{0,1:T(8,128)(2,1)}, bf16[1024,640]{0,1:T(8,128)(2,1)}, u32[]{:S(2)}, u32[]{:S(2)}) collective-permute-start(bf16[1024,640]{0,1:T(8,128)(2,1)} %fusion.22), channel_id=1, source_target_pairs={{0,1},{1,0},{2,3},{3,2},{4,5},{5,4},{6,7},{7,6},{8,9},{9,8},{10,11... | collective-permute-start | bytes 3932168 | tf_op jit(solution)/shard_map/ppermute | solution.py:87
  13.3 71.8 %collective-permute-start.4 = (bf16[1024,640]{0,1:T(8,128)(2,1)}, bf16[1024,640]{0,1:T(8,128)(2,1)}, u32[]{:S(2)}, u32[]{:S(2)}) collective-permute-start(bf16[1024,640]{0,1:T(8,128)(2,1)} %fusion.21), channel_id=1, source_target_pairs={{0,1},{1,0},{2,3},{3,2},{4,5},{5,4},{6,7},{7,6},{8,9},{9,8},{10,11... | collective-permute-start | bytes 3932168 | tf_op jit(solution)/shard_map/ppermute | solution.py:87
  14.0 5.6 %copy-start.4 = (bf16[1,64,5120]{2,1,0:T(8,128)(2,1)S(1)}, bf16[1,64,5120]{2,1,0:T(8,128)(2,1)}, u32[]{:S(2)}) copy-start(bf16[1,64,5120]{2,1,0:T(8,128)(2,1)} %param.20) | copy-start | bytes 1966084
  14.0 5.7 %copy-start.5 = (bf16[1,5120,64]{1,2,0:T(8,128)(2,1)S(1)}, bf16[1,5120,64]{1,2,0:T(8,128)(2,1)}, u32[]{:S(2)}) copy-start(bf16[1,5120,64]{1,2,0:T(8,128)(2,1)} %param.19) | copy-start | bytes 1966084
  17.6 2.2 copy-start.3
  17.6 111.3 %collective-permute-start.3 = (bf16[1024,640]{0,1:T(8,128)(2,1)}, bf16[1024,640]{0,1:T(8,128)(2,1)}, u32[]{:S(2)}, u32[]{:S(2)}) collective-permute-start(bf16[1024,640]{0,1:T(8,128)(2,1)} %fusion.20), channel_id=1, source_target_pairs={{0,1},{1,0},{2,3},{3,2},{4,5},{5,4},{6,7},{7,6},{8,9},{9,8},{10,11... | collective-permute-start | bytes 3932168 | tf_op jit(solution)/shard_map/ppermute | solution.py:87
  22.0 96.2 %all-to-all-start = ((bf16[8,1,64,2176]{3,2,1,0:T(8,128)(2,1)}), bf16[8,1,64,2176]{3,2,1,0:T(8,128)(2,1)S(1)}, u32[]{:S(2)}, u32[]{:S(2)}) async-start(bf16[8,1,64,2176]{3,2,1,0:T(8,128)(2,1)} %copy.25), calls=%async_computation | async-start | bytes 4456448 | tf_op jit(solution)/shard_map/all_to_all | solution.py:103
  27.3 117.6 %collective-permute-start = (bf16[1,5120,64]{1,2,0:T(8,128)(2,1)}, bf16[1,5120,64]{1,2,0:T(8,128)(2,1)}, u32[]{:S(2)}, u32[]{:S(2)}) collective-permute-start(bf16[1,5120,64]{1,2,0:T(8,128)(2,1)} %param.17), channel_id=1, source_target_pairs={{0,8},{8,0},{1,9},{9,1},{2,10},{10,2},{3,11},{11,3},{4,12},{12,4},... | collective-permute-start | bytes 1966088 | tf_op jit(solution)/shard_map/ppermute | solution.py:106
  44.2 18.9 %copy-start.9 = (s32[2,6]{1,0:T(2,128)S(1)}, s32[2,6]{1,0:T(2,128)}, u32[]{:S(2)}) copy-start(s32[2,6]{1,0:T(2,128)} %param.23) | copy-start | bytes 148
  44.2 19.6 %copy-start.10 = (s32[16]{0:T(128)S(1)}, s32[16]{0:T(128)}, u32[]{:S(2)}) copy-start(s32[16]{0:T(128)} %param.24) | copy-start | bytes 196
  56.9 34.7 %collective-permute-start.6 = (bf16[1024,640]{0,1:T(8,128)(2,1)}, bf16[1024,640]{0,1:T(8,128)(2,1)}, u32[]{:S(2)}, u32[]{:S(2)}) collective-permute-start(bf16[1024,640]{0,1:T(8,128)(2,1)} %get-tuple-element.20), channel_id=1, source_target_pairs={{0,2},{1,3},{8,10},{9,11},{16,18},{17,19},{24,26},{25,27}} | collective-permute-start | bytes 3932168 | tf_op jit(solution)/shard_map/ppermute | solution.py:100
  59.9 31.7 %collective-permute-start.9 = (bf16[1024,640]{0,1:T(8,128)(2,1)}, bf16[1024,640]{0,1:T(8,128)(2,1)}, u32[]{:S(2)}, u32[]{:S(2)}) collective-permute-start(bf16[1024,640]{0,1:T(8,128)(2,1)} %get-tuple-element.20), channel_id=1, source_target_pairs={{6,4},{7,5},{14,12},{15,13},{22,20},{23,21},{30,28},{31,29}} | collective-permute-start | bytes 3932168 | tf_op jit(solution)/shard_map/ppermute | solution.py:101
  65.5 26.1 %copy-start.1 = (f32[1024,640]{0,1:T(8,128)S(1)}, f32[1024,640]{0,1:T(8,128)}, u32[]{:S(2)}) copy-start(f32[1024,640]{0,1:T(8,128)} %get-tuple-element.21) | copy-start | bytes 7864324
  87.9 8.0 %copy-start.2 = (f32[1024,640]{0,1:T(8,128)}, f32[1024,640]{0,1:T(8,128)S(1)}, u32[]{:S(2)}) copy-start(f32[1024,640]{0,1:T(8,128)S(1)} %bitcast_add_fusion.3) | copy-start | bytes 7864324
  95.9 34.8 %collective-permute-start.10 = (bf16[1024,640]{0,1:T(8,128)(2,1)}, bf16[1024,640]{0,1:T(8,128)(2,1)}, u32[]{:S(2)}, u32[]{:S(2)}) collective-permute-start(bf16[1024,640]{0,1:T(8,128)(2,1)} %get-tuple-element.15), channel_id=1, source_target_pairs={{4,2},{5,3},{6,4},{7,5},{12,10},{13,11},{14,12},{15,13},{20,18},{2... | collective-permute-start | bytes 3932168 | tf_op jit(solution)/shard_map/ppermute | solution.py:101
  97.6 33.1 %collective-permute-start.7 = (bf16[1024,640]{0,1:T(8,128)(2,1)}, bf16[1024,640]{0,1:T(8,128)(2,1)}, u32[]{:S(2)}, u32[]{:S(2)}) collective-permute-start(bf16[1024,640]{0,1:T(8,128)(2,1)} %get-tuple-element.14), channel_id=1, source_target_pairs={{0,2},{1,3},{2,4},{3,5},{8,10},{9,11},{10,12},{11,13},{16,18},{17,... | collective-permute-start | bytes 3932168 | tf_op jit(solution)/shard_map/ppermute | solution.py:100
  118.2 35.2 %collective-permute-start.1 = (bf16[8,64,2176]{2,1,0:T(8,128)(2,1)S(1)}, bf16[8,64,2176]{2,1,0:T(8,128)(2,1)}, u32[]{:S(2)}, u32[]{:S(2)}) collective-permute-start(bf16[8,64,2176]{2,1,0:T(8,128)(2,1)S(1)} %bitcast.110), channel_id=1, source_target_pairs={{0,8},{8,0},{1,9},{9,1},{2,10},{10,2},{3,11},{11,3},{4,12},{12,4},... | collective-permute-start | bytes 6684680 | tf_op jit(solution)/shard_map/ppermute | solution.py:105
  128.9 16.1 %copy-start.7 = (pred[1024,2]{0,1:T(4,128)(4,1)S(1)}, pred[1024,2]{0,1:T(4,128)(4,1)}, u32[]{:S(2)}) copy-start(pred[1024,2]{0,1:T(4,128)(4,1)} %broadcast_compare_fusion.1) | copy-start | bytes 6148
  128.9 16.1 %copy-start.8 = (bf16[1,5120,64]{1,2,0:T(8,128)(2,1)S(1)}, bf16[1,5120,64]{1,2,0:T(8,128)(2,1)}, u32[]{:S(2)}) copy-start(bf16[1,5120,64]{1,2,0:T(8,128)(2,1)} %param.17) | copy-start | bytes 1966084
  128.9 80.9 %collective-permute-start.2 = (bf16[1024,640]{0,1:T(8,128)(2,1)}, bf16[1024,640]{0,1:T(8,128)(2,1)}, u32[]{:S(2)}, u32[]{:S(2)}) collective-permute-start(bf16[1024,640]{0,1:T(8,128)(2,1)} %fusion.19), channel_id=1, source_target_pairs={{0,1},{1,0},{2,3},{3,2},{4,5},{5,4},{6,7},{7,6},{8,9},{9,8},{10,11... | collective-permute-start | bytes 3932168 | tf_op jit(solution)/shard_map/ppermute | solution.py:87
  138.0 71.9 %collective-permute-start.11 = (bf16[1024,640]{0,1:T(8,128)(2,1)}, bf16[1024,640]{0,1:T(8,128)(2,1)}, u32[]{:S(2)}, u32[]{:S(2)}) collective-permute-start(bf16[1024,640]{0,1:T(8,128)(2,1)} %get-tuple-element.13), channel_id=1, source_target_pairs={{2,0},{3,1},{4,2},{5,3},{6,4},{7,5},{10,8},{11,9},{12,10},{13,11},... | collective-permute-start | bytes 3932168 | tf_op jit(solution)/shard_map/ppermute | solution.py:101
  139.3 14.2 %copy-start.6 = (pred[1024,16]{0,1:T(8,128)(4,1)S(1)}, pred[1024,16]{0,1:T(8,128)(4,1)}, u32[]{:S(2)}) copy-start(pred[1024,16]{0,1:T(8,128)(4,1)} %broadcast_compare_fusion) | copy-start | bytes 49156
  139.3 70.6 %collective-permute-start.8 = (bf16[1024,640]{0,1:T(8,128)(2,1)}, bf16[1024,640]{0,1:T(8,128)(2,1)}, u32[]{:S(2)}, u32[]{:S(2)}) collective-permute-start(bf16[1024,640]{0,1:T(8,128)(2,1)} %get-tuple-element.12), channel_id=1, source_target_pairs={{0,2},{1,3},{2,4},{3,5},{4,6},{5,7},{8,10},{9,11},{10,12},{11,13},... | collective-permute-start | bytes 3932168 | tf_op jit(solution)/shard_map/ppermute | solution.py:100

commit v2 on v1

v2 whole, which is shorter than its diff:
```python
import jax
import jax.numpy as jnp
from jax import lax
from jax.sharding import PartitionSpec as P


def chunk_order(depth):
    rows = []
    for z in range(depth):
        row = []
        for s in range(depth - 1):
            for d, ok in ((z + depth - 1 - s, s >= z), (z - depth + 1 + s, s >= depth - 1 - z)):
                if ok:
                    row.append(d)
        rows.append(row + [z])
    return rows


def token_rows(seg_len, seg_use, row_of_use, tok_rows):
    count = seg_len.shape[0]
    order = jnp.arange(count, dtype=jnp.int32)
    ends = jnp.sum(jnp.where(order[None, :] <= order[:, None], seg_len[None, :], 0), axis=1)
    used = jnp.arange(row_of_use.shape[0], dtype=jnp.int32)
    seg_row = jnp.sum(jnp.where(seg_use[:, None] == used[None, :], row_of_use[None, :], 0), axis=1)
    positions = jnp.arange(tok_rows, dtype=jnp.int32)
    inside = (positions[:, None] >= (ends - seg_len)[None, :]) & (positions[:, None] < ends[None, :])
    return jnp.sum(jnp.where(inside, seg_row[None, :], 0), axis=1)


def shards(
    hidden,
    context,
    w_qkv,
    w_out,
    a_qkv,
    b_qkv,
    a_out,
    b_out,
    seg_len,
    seg_use,
    used_list,
    adapter_slot,
):
    f32, bf16 = jnp.float32, jnp.bfloat16
    tensor_size = lax.axis_size("tensor")
    dp_size = lax.axis_size("dp")
    t = lax.axis_index("tensor")
    dp_rank = lax.axis_index("dp")
    tok_rows, model_width = hidden.shape
    owned, _, rank = a_qkv.shape
    out_part = model_width // tensor_size
    qkv_part = b_qkv.shape[2] // tensor_size
    depth = tensor_size // 2
    z, y = t // 2, t % 2

    used = used_list[dp_rank][:, None] == jnp.arange(adapter_slot.shape[0], dtype=jnp.int32)[None, :]
    row_of_use = jnp.sum(jnp.where(used, adapter_slot[None, :], 0), axis=1)
    store_row = token_rows(seg_len[0], seg_use[0], row_of_use, tok_rows)

    order = jnp.asarray(chunk_order(depth), jnp.int32)[z]
    swap = [(i, i ^ 1) for i in range(tensor_size)]
    both = [(0, 1), (1, 0)]
    barrier = lax.optimization_barrier

    row_half = out_part // dp_size
    my_rows = lax.dynamic_slice_in_dim(w_out, dp_rank * row_half, row_half, 0)

    def cols(weights, d, side):
        return lax.dynamic_slice_in_dim(weights, (2 * d + side) * out_part, out_part, 1)

    def trade(pieces):
        sent = jnp.concatenate([cols(my_rows, order[k], 1 - y) for k in pieces], axis=1)
        mine = lax.ppermute(sent, "tensor", swap)
        other = lax.ppermute(mine, "dp", both)
        return jnp.concatenate(
            (jnp.where(dp_rank == 0, mine, other), jnp.where(dp_rank == 0, other, mine)), axis=0
        )

    context_two = jnp.concatenate((context, lax.ppermute(context, "tensor", swap)), axis=1)
    w_first = trade([0])
    w_rest = trade(list(range(1, depth)))

    def reduced_chunk(k):
        theirs = w_first if k == 0 else w_rest[:, (k - 1) * out_part : k * out_part]
        weights = jnp.concatenate((cols(w_out, order[k], y), theirs), axis=0)
        return jnp.dot(context_two, weights, preferred_element_type=f32)

    def split(maps, part):
        return jnp.transpose(maps.reshape(owned, rank, tensor_size, part), (2, 0, 1, 3))

    def spread_rows(sent):
        got = lax.all_to_all(sent, "tensor", split_axis=0, concat_axis=0, tiled=True)
        got = got.reshape((-1,) + got.shape[2:])
        return jnp.concatenate((got, lax.ppermute(got, "dp", both)), axis=0)

    a_other = lax.ppermute(a_qkv, "dp", both)
    down_out = spread_rows(split(jnp.transpose(a_out, (0, 2, 1)), out_part))
    up_sent = jnp.concatenate((split(b_out, out_part), split(b_qkv, qkv_part)), axis=3)
    up_maps = spread_rows(up_sent)
    up_out = up_maps[:, :, :out_part].reshape(-1, out_part)
    up_qkv = up_maps[:, :, out_part:].reshape(-1, qkv_part)

    half = tensor_size * owned
    first, second = dp_rank * half, (1 - dp_rank) * half

    def lane_mask(rows):
        return store_row[:, None] == jnp.repeat(rows, rank)[None, :]

    rows = jnp.arange(half, dtype=jnp.int32)
    row_mask = lane_mask(jnp.concatenate((first + rows, second + rows)))
    own = jnp.arange(owned, dtype=jnp.int32) + t * owned
    own_mask = lane_mask(jnp.concatenate((first + own, second + own)))

    def pick(products, mask):
        kept = jnp.where(mask, products, 0.0)
        wide = sum(kept[:, i : i + 2 * rank] for i in range(0, kept.shape[1], 2 * rank))
        return wide[:, :rank] + wide[:, rank:]

    a_two = jnp.concatenate((a_qkv, a_other), axis=0)
    low_a = pick(
        jnp.dot(hidden, jnp.transpose(a_two, (1, 0, 2)).reshape(model_width, -1), preferred_element_type=f32),
        own_mask,
    )
    low_b = pick(
        lax.dot_general(
            context,
            down_out.reshape(-1, out_part),
            (((1,), (1,)), ((), ())),
            preferred_element_type=f32,
        ),
        row_mask,
    )
    low = jnp.concatenate((low_a, low_b), axis=1)
    step = 1
    while step < tensor_size:
        pairs = [(i, i ^ step) for i in range(tensor_size)]
        low = low + lax.ppermute(low.astype(bf16), "tensor", pairs).astype(f32)
        step = 2 * step
    low = low.astype(bf16)

    def expand(low_rank, maps):
        twice = jnp.concatenate((low_rank, low_rank), axis=1)
        spread = jnp.concatenate([twice] * (row_mask.shape[1] // (2 * rank)), axis=1)
        spread = jnp.where(row_mask, spread, jnp.zeros((), bf16))
        return jnp.dot(spread, maps, preferred_element_type=f32)

    reduced, up, down, late = [], None, None, hidden

    def chosen(d):
        value = reduced[0]
        for k in range(1, len(reduced)):
            value = jnp.where(order[k] == d, reduced[k], value)
        return value

    for s in range(depth - 1):
        reduced.append(reduced_chunk(s))
        to_up, to_down = chosen(z + depth - 1 - s), chosen(z - depth + 1 + s)
        if s > 0:
            to_up, to_down = to_up + up.astype(f32), to_down + down.astype(f32)
        to_up, to_down = to_up.astype(bf16), to_down.astype(bf16)
        if s == 0:
            to_up, to_down, late = barrier((to_up, to_down, late))
        up_pairs = [(2 * i + j, 2 * i + 2 + j) for i in range(s + 1) for j in range(2)]
        down_pairs = [
            (2 * i + j, 2 * i - 2 + j) for i in range(depth - 1 - s, depth) for j in range(2)
        ]
        up = lax.ppermute(to_up, "tensor", up_pairs)
        down = lax.ppermute(to_down, "tensor", down_pairs)

    base_qkv = jnp.dot(late, w_qkv, preferred_element_type=f32)
    qkv = (base_qkv + expand(low[:, :rank], up_qkv)).astype(bf16)
    here = reduced_chunk(depth - 1) + expand(low[:, rank:], up_out)
    qkv, here = barrier((qkv, here))
    attn_out = (here + up.astype(f32) + down.astype(f32)).astype(bf16)
    return (qkv, attn_out)


def solution(mesh):
    placed = (
        P(("groups", "dp"), None),
        P(("groups", "dp"), "tensor"),
        P(None, "tensor"),
        P("tensor", None),
        P(("dp", "tensor"), None, None),
        P(("dp", "tensor"), None, None),
        P(("dp", "tensor"), None, None),
        P(("dp", "tensor"), None, None),
        P(("groups", "dp"), None),
        P(("groups", "dp"), None),
        P("groups", None),
        P(),
    )
    return jax.shard_map(
        shards,
        mesh=mesh,
        in_specs=placed,
        out_specs=(P(("groups", "dp"), "tensor"), P(("groups", "dp"), "tensor")),
        check_vma=False,
    )
```

time: 225 us -> 248 us (1.10)
  waiting for transfers between devices: 41.6 us -> 108 us
  blocking collectives: 52.7 us -> 0 us
  matrix products: 70.3 us -> 46.8 us
  local copies, waits for them, and re-layouts: 6.14 us -> 28.2 us
  starting transfers between devices: 30.6 us -> 41.6 us
    psum x1 -> x0, blocking collectives: 52.7 us -> none  [shards(): lax.psum((pick(low_a, own_mask), pick(low_b, row_mask)), 'tensor')]
    ppermute x11 -> x16, waiting for transfers between devices: 31.3 us -> 80.7 us  [the longest x3 35.1 us: shards(): up = lax.ppermute(to_up, 'tensor', up_pairs)]
    dot_general x13 -> x9, matrix products: 70.3 us -> 46.8 us  [the longest x1 14.8 us: shards(): base_qkv = jnp.dot(late, w_qkv, preferred_element_type=f32)]
    all_to_all x1 -> x2, waiting for transfers between devices: 10.3 us -> 27.7 us  [spread_rows(): lax.all_to_all(sent, 'tensor', split_axis=0, concat_axis=0, tiled=True)]
    unnamed x26 -> x81, local copies, waits for them, and re-layouts: 2.77 us -> 14.7 us
    dynamic_slice x0 -> x2, local copies, waits for them, and re-layouts: none -> 6.27 us  [cols(): lax.dynamic_slice_in_dim(weights, (2 * d + side) * out_part, out_part, 1)]
    all_to_all x1 -> x2, starting transfers between devices: 5.29 us -> 10.9 us  [spread_rows(): lax.all_to_all(sent, 'tensor', split_axis=0, concat_axis=0, tiled=True)]
    ppermute x11 -> x16, starting transfers between devices: 25.3 us -> 30.6 us  [the longest x3 11.4 us: shards(): up = lax.ppermute(to_up, 'tensor', up_pairs)]
  transfers between devices with their start and end apart: 13 -> 19, of which waited for: 4 -> 8; matrix products, arithmetic and copies ran while one was open for 32% -> 33% of each run, Pallas kernels for 0% -> 0%
where the time goes in v2:
time: 248 us; the launch traced here: 247 us
  waiting for transfers between devices  108 us (44%)
  matrix products  46.8 us (19%)
  starting transfers between devices  41.6 us (17%)
  local copies, waits for them, and re-layouts  28.2 us (11%)
  other arithmetic  14.2 us (6%)
  between operations  7.5 us (3%)
    ppermute x3, waiting for transfers between devices, shards(): up = lax.ppermute(to_up, 'tensor', up_pairs)  35.1 us
    all_to_all x2, waiting for transfers between devices, spread_rows(): lax.all_to_all(sent, 'tensor', split_axis=0, concat_axis=0, tiled=True)  27.7 us
    ppermute x2, waiting for transfers between devices, trade(): mine = lax.ppermute(sent, 'tensor', swap)  21 us
    ppermute x3, waiting for transfers between devices, shards(): low = low + lax.ppermute(low.astype(bf16), 'tensor', pairs).astype(f32)  20.3 us
    dot_general x1, matrix products, shards(): base_qkv = jnp.dot(late, w_qkv, preferred_element_type=f32)  14.8 us
    unnamed x81, local copies, waits for them, and re-layouts  14.7 us
    dot_general x4, matrix products, reduced_chunk(): return jnp.dot(context_two, weights, preferred_element_type=f32)  12.8 us
    ppermute x3, starting transfers between devices, shards(): up = lax.ppermute(to_up, 'tensor', up_pairs)  11.4 us
  transfers between devices with their start and end apart: 19, of which 8 were waited for; matrix products, arithmetic and copies ran while one was open for 33% of the time, Pallas kernels for 0%

profile of v2, /device:TPU:0, one launch (start us, length us, event | category | flops | bytes accessed | tf_op | source)
XLA Modules:
  0.0 246.8 jit_solution(16856951899374054261)
XLA Ops:
  4.5 2.6 %fusion.46 = (bf16[320,640]{1,0:T(8,128)(2,1)S(1)}, bf16[320,640]{1,0:T(8,128)(2,1)S(1)}, bf16[320,640]{1,0:T(8,128)(2,1)S(1)}, bf16[320,640]{1,0:T(8,128)(2,1)S(1)}) fusion(bf16[640,5120]{1,0:T(8,128)(2,1)} %param.16, s32[]{:T(128)S(6)} %select_n.153, s32[]{:T(128)S(6)} %select_n.169, s32[]{:T(128)S(6)} %select_n.173, s32[]{:T(128)S(6)} %select_n.171, ...), kind=kLoop, calls=%fused_computation.139 | loop fusion | bytes 3276820 | tf_op jit(solution)/shard_map/dynamic_slice | solution.py:69
  8.2 3.0 %collective-permute-start.9 = (bf16[320,1920]{1,0:T(8,128)(2,1)}, bf16[320,1920]{1,0:T(8,128)(2,1)}, u32[]{:S(2)}, u32[]{:S(2)}) collective-permute-start(bf16[320,1920]{1,0:T(8,128)(2,1)} %pad_maximum_fusion.5), channel_id=1, source_target_pairs={{0,1},{1,0},{2,3},{3,2},{4,5},{5,4},{6,7},{7,6},{8,9},{9,8},{10,11... | collective-permute-start | bytes 3686408 | tf_op jit(solution)/shard_map/ppermute | solution.py:73
  11.2 2.0 collective-permute-start
  14.4 4.9 %all-to-all-start = ((bf16[8,1,64,640]{3,2,1,0:T(8,128)(2,1)}), bf16[8,1,64,640]{3,2,1,0:T(8,128)(2,1)S(1)}, u32[]{:S(2)}, u32[]{:S(2)}) async-start(bf16[8,1,64,640]{3,2,1,0:T(8,128)(2,1)} %copy.20), calls=%async_computation | async-start | bytes 1310720 | tf_op jit(solution)/shard_map/all_to_all | solution.py:92
  26.2 2.6 %constant_dynamic-update-slice_fusion.1 = bf16[1024,1280]{1,0:T(8,128)(2,1)} fusion(bf16[1024,640]{1,0:T(8,128)(2,1)} %param.14), kind=kLoop, calls=%fused_computation.80 | loop fusion | bytes 2621440
  28.7 3.7 %constant_dynamic-slice_fusion.1 = (bf16[640,640]{1,0:T(8,128)(2,1)}, bf16[640,640]{1,0:T(8,128)(2,1)}, bf16[640,640]{1,0:T(8,128)(2,1)}, bf16[640,640]{1,0:T(8,128)(2,1)}) fusion(bf16[640,5120]{1,0:T(8,128)(2,1)} %param.16, s32[]{:T(128)S(6)} %select_n.178, s32[]{:T(128)S(6)} %select_n.166, s32[]{:T(128)S(6)} %select_n.150, s32[]{:T(128)S(6)} %select_n.180), kind=kLoop, calls=%fused_computation.121 | loop fusion | bytes 6553616 | tf_op jit(solution)/shard_map/dynamic_slice | solution.py:69
  32.4 21.0 %collective-permute-done.1 = bf16[320,640]{1,0:T(8,128)(2,1)} collective-permute-done((bf16[320,640]{1,0:T(8,128)(2,1)S(1)}, bf16[320,640]{1,0:T(8,128)(2,1)}, u32[]{:S(2)}, u32[]{:S(2)}) %collective-permute-start.1) | collective-permute-done | bytes 409632 | tf_op jit(solution)/shard_map/ppermute | solution.py:73
  54.6 27.7 %all-to-all-done = bf16[8,1,64,640]{3,2,1,0:T(8,128)(2,1)S(1)} async-done(((bf16[8,1,64,640]{3,2,1,0:T(8,128)(2,1)}), bf16[8,1,64,640]{3,2,1,0:T(8,128)(2,1)S(1)}, u32[]{:S(2)}, u32[]{:S(2)}) %all-to-all-start) | async-done | bytes 655392 | tf_op jit(solution)/shard_map/all_to_all | solution.py:92
  82.3 6.1 %all-to-all-start.1 = ((bf16[8,1,64,1536]{3,2,1,0:T(8,128)(2,1)}), bf16[8,1,64,1536]{3,2,1,0:T(8,128)(2,1)S(1)}, u32[]{:S(2)}, u32[]{:S(2)}) async-start(bf16[8,1,64,1536]{3,2,1,0:T(8,128)(2,1)} %copy.21), calls=%async_computation.1 | async-start | bytes 3145728 | tf_op jit(solution)/shard_map/all_to_all | solution.py:92
  88.4 7.7 %fusion.29 = f32[1024,128]{0,1:T(8,128)S(1)} fusion(bf16[5120,128]{0,1:T(8,128)(2,1)S(1)} %bitcast.72, bf16[1024,5120]{1,0:T(8,128)(2,1)} %param.13, s32[1024]{0:T(1024)S(1)} %select_reduce_fusion, s32[128]{0:T(128)S(1)} %eq.100), kind=kOutput, calls=%fused_computation.50 | convolution fusion | flops 1342439424 | bytes 12325376 | tf_op jit(solution)/shard_map/dot_general | solution.py:121
  99.7 4.0 %compare_select_fusion.2 = f32[1024,1024]{0,1:T(8,128)S(1)} fusion(bf16[1024,640]{1,0:T(8,128)(2,1)S(1)} %bitcast.79, bf16[1024,640]{1,0:T(8,128)(2,1)} %param.14, s32[1024]{0:T(1024)S(1)} %select_reduce_fusion, s32[1024]{0:T(1024)S(1)} %eq.96), kind=kOutput, calls=%fused_computation.2 | convolution fusion | flops 1344274432 | bytes 6823936 | tf_op jit(solution)/shard_map/dot_general | solution.py:125
  104.2 2.1 collective-permute-start.5
  106.2 2.2 fusion.48
  108.5 3.5 %collective-permute-start.11 = (bf16[1024,640]{1,0:T(8,128)(2,1)S(1)}, bf16[1024,640]{1,0:T(8,128)(2,1)S(1)}, u32[]{:S(2)}, u32[]{:S(2)}) collective-permute-start(bf16[1024,640]{1,0:T(8,128)(2,1)S(1)} %get-tuple-element.11), channel_id=1, source_target_pairs={{0,2},{1,3},{8,10},{9,11},{16,18},{17,19},{24,26},{25,27}} | collective-permute-start | bytes 3932168 | tf_op jit(solution)/shard_map/ppermute | solution.py:167
  112.8 4.5 %collective-permute-done.5 = bf16[1024,128]{0,1:T(8,128)(2,1)S(1)} collective-permute-done((bf16[1024,128]{0,1:T(8,128)(2,1)S(1)}, bf16[1024,128]{0,1:T(8,128)(2,1)S(1)}, u32[]{:S(2)}, u32[]{:S(2)}) %collective-permute-start.5) | collective-permute-done | bytes 262176 | tf_op jit(solution)/shard_map/ppermute | solution.py:137
  117.4 2.6 %collective-permute-start.6 = (bf16[1024,128]{0,1:T(8,128)(2,1)S(1)}, bf16[1024,128]{0,1:T(8,128)(2,1)S(1)}, u32[]{:S(2)}, u32[]{:S(2)}) collective-permute-start(bf16[1024,128]{0,1:T(8,128)(2,1)S(1)} %fusion.37), channel_id=1, source_target_pairs={{0,2},{1,3},{2,0},{3,1},{4,6},{5,7},{6,4},{7,5},{8,10},{9,11},{10,... | collective-permute-start | bytes 786440 | tf_op jit(solution)/shard_map/ppermute | solution.py:137
  120.0 14.8 %fusion.49 = f32[1024,896]{1,0:T(8,128)} fusion(bf16[1024,5120]{1,0:T(8,128)(2,1)S(1)} %bitcast.71, bf16[5120,896]{1,0:T(8,128)(2,1)} %param.15), kind=kOutput, calls=%fused_computation.142 | convolution fusion | flops 9395240960 | bytes 23330816 | tf_op jit(solution)/shard_map/dot_general | solution.py:170
  134.9 11.9 %collective-permute-done.6 = bf16[1024,128]{0,1:T(8,128)(2,1)S(1)} collective-permute-done((bf16[1024,128]{0,1:T(8,128)(2,1)S(1)}, bf16[1024,128]{0,1:T(8,128)(2,1)S(1)}, u32[]{:S(2)}, u32[]{:S(2)}) %collective-permute-start.6) | collective-permute-done | bytes 262176 | tf_op jit(solution)/shard_map/ppermute | solution.py:137
  146.9 4.6 %collective-permute-start.7 = (bf16[1024,128]{0,1:T(8,128)(2,1)S(1)}, bf16[1024,128]{0,1:T(8,128)(2,1)S(1)}, u32[]{:S(2)}, u32[]{:S(2)}) collective-permute-start(bf16[1024,128]{0,1:T(8,128)(2,1)S(1)} %fusion.35), channel_id=1, source_target_pairs={{0,4},{1,5},{2,6},{3,7},{4,0},{5,1},{6,2},{7,3},{8,12},{9,13},{10,... | collective-permute-start | bytes 786440 | tf_op jit(solution)/shard_map/ppermute | solution.py:137
  154.4 3.7 %fusion.21 = f32[1024,640]{1,0:T(8,128)} fusion(bf16[1024,1280]{1,0:T(8,128)(2,1)S(1)} %constant_dynamic-update-slice_fusion, bf16[640,640]{1,0:T(8,128)(2,1)S(1)} %get-tuple-element.24, bf16[640,640]{1,0:T(8,128)(2,1)S(1)} %copy-done.6), kind=kOutput, calls=%fused_computation.36 | convolution fusion | flops 1680998400 | bytes 6881280 | tf_op jit(solution)/shard_map/dot_general | solution.py:86
  158.1 3.9 %collective-permute-done.7 = bf16[1024,128]{0,1:T(8,128)(2,1)S(1)} collective-permute-done((bf16[1024,128]{0,1:T(8,128)(2,1)S(1)}, bf16[1024,128]{0,1:T(8,128)(2,1)S(1)}, u32[]{:S(2)}, u32[]{:S(2)}) %collective-permute-start.7) | collective-permute-done | bytes 262176 | tf_op jit(solution)/shard_map/ppermute | solution.py:137
  169.1 4.7 %add_convert_fusion.5 = (bf16[1024,640]{1,0:T(8,128)(2,1)}, bf16[1024,640]{1,0:T(8,128)(2,1)}, f32[1024,640]{1,0:T(8,128)}) fusion(bf16[1024,640]{1,0:T(8,128)(2,1)S(1)} %collective-permute-done.11, f32[1024,640]{1,0:T(8,128)S(1)} %get-tuple-element.37, pred[]{:T(512)S(6)} %eq.105, bf16[1024,640]{1,0:T(8,128)(2,1)S(1)} %collective-permute-done.14, ...), kind=kOutput, calls=%fused_computation.14 | convolution fusion | flops 1687879680 | bytes 16384002 | tf_op jit(solution)/shard_map/dot_general | solution.py:86
  175.2 1.8 collective-permute-start.15
  180.9 22.5 %collective-permute-done.12 = bf16[1024,640]{1,0:T(8,128)(2,1)S(1)} collective-permute-done((bf16[1024,640]{1,0:T(8,128)(2,1)}, bf16[1024,640]{1,0:T(8,128)(2,1)S(1)}, u32[]{:S(2)}, u32[]{:S(2)}) %collective-permute-start.12) | collective-permute-done | bytes 1310752 | tf_op jit(solution)/shard_map/ppermute | solution.py:167
  203.4 4.6 %add_convert_fusion.4 = (bf16[1024,640]{1,0:T(8,128)(2,1)S(1)}, bf16[1024,640]{1,0:T(8,128)(2,1)S(1)}) fusion(bf16[1024,640]{1,0:T(8,128)(2,1)S(1)} %collective-permute-done.12, f32[1024,640]{1,0:T(8,128)} %fusion.21, f32[1024,640]{1,0:T(8,128)} %get-tuple-element.38, f32[1024,640]{1,0:T(8,128)} %copy-done.2, pred[]{:T(512)S(6)} %eq.104, pred[]{:T(512)S(6)} %eq.103, ...), kind=kLoop, calls=%fused_computation.13 | loop fusion | flops 6553600 | bytes 13107204 | tf_op jit(solution)/shard_map/convert_element_type | solution.py:160
  208.0 6.5 %collective-permute-start.13 = (bf16[1024,640]{1,0:T(8,128)(2,1)S(1)}, bf16[1024,640]{1,0:T(8,128)(2,1)S(1)}, u32[]{:S(2)}, u32[]{:S(2)}) collective-permute-start(bf16[1024,640]{1,0:T(8,128)(2,1)S(1)} %get-tuple-element.12), channel_id=1, source_target_pairs={{0,2},{1,3},{2,4},{3,5},{4,6},{5,7},{8,10},{9,11},{10,12},{11,13},... | collective-permute-start | bytes 3932168 | tf_op jit(solution)/shard_map/ppermute | solution.py:167
  214.6 1.6 collective-permute-start.16
  216.4 2.0 fusion.1
  220.7 2.2 fusion.26
  222.9 5.5 %add_convert_fusion = bf16[1024,896]{1,0:T(8,128)(2,1)} fusion(f32[1024,896]{1,0:T(8,128)S(1)} %copy-done.20, bf16[1024,896]{1,0:T(8,128)(2,1)S(1)} %bitcast.78, bf16[1024,1024]{0,1:T(8,128)(2,1)} %constant_dynamic-update-slice_fusion.2, s32[1024]{0:T(1024)S(1)} %select_reduce_fusion, s32[1024]{0:T(1024)S(1)} %eq.96), kind=kOutput, calls=%fused_computation.3 | convolution fusion | flops 1882980352 | bytes 9445376 | tf_op jit(solution)/shard_map/dot_general | solution.py:145
  228.4 12.6 %collective-permute-done.13 = bf16[1024,640]{1,0:T(8,128)(2,1)S(1)} collective-permute-done((bf16[1024,640]{1,0:T(8,128)(2,1)S(1)}, bf16[1024,640]{1,0:T(8,128)(2,1)S(1)}, u32[]{:S(2)}, u32[]{:S(2)}) %collective-permute-start.13) | collective-permute-done | bytes 1310752 | tf_op jit(solution)/shard_map/ppermute | solution.py:167
  241.0 4.3 %collective-permute-done.16 = bf16[1024,640]{1,0:T(8,128)(2,1)S(1)} collective-permute-done((bf16[1024,640]{1,0:T(8,128)(2,1)S(1)}, bf16[1024,640]{1,0:T(8,128)(2,1)S(1)}, u32[]{:S(2)}, u32[]{:S(2)}) %collective-permute-start.16) | collective-permute-done | bytes 1310752 | tf_op jit(solution)/shard_map/ppermute | solution.py:168
  (140 shorter events, 32.0 us)
Async XLA Ops:
  0.6 25.1 %copy-start = (s32[2,6]{1,0:T(2,128)S(1)}, s32[2,6]{1,0:T(2,128)}, u32[]{:S(2)}) copy-start(s32[2,6]{1,0:T(2,128)} %param.23) | copy-start | bytes 148
  4.5 8.8 %copy-start.13 = (bf16[1,5120,64]{1,2,0:T(8,128)(2,1)S(1)}, bf16[1,5120,64]{1,2,0:T(8,128)(2,1)}, u32[]{:S(2)}) copy-start(bf16[1,5120,64]{1,2,0:T(8,128)(2,1)} %param.19) | copy-start | bytes 1966084
  8.2 89.2 %collective-permute-start.9 = (bf16[320,1920]{1,0:T(8,128)(2,1)}, bf16[320,1920]{1,0:T(8,128)(2,1)}, u32[]{:S(2)}, u32[]{:S(2)}) collective-permute-start(bf16[320,1920]{1,0:T(8,128)(2,1)} %pad_maximum_fusion.5), channel_id=1, source_target_pairs={{0,1},{1,0},{2,3},{3,2},{4,5},{5,4},{6,7},{7,6},{8,9},{9,8},{10,11... | collective-permute-start | bytes 3686408 | tf_op jit(solution)/shard_map/ppermute | solution.py:73
  11.2 42.2 %collective-permute-start.1 = (bf16[320,640]{1,0:T(8,128)(2,1)S(1)}, bf16[320,640]{1,0:T(8,128)(2,1)}, u32[]{:S(2)}, u32[]{:S(2)}) collective-permute-start(bf16[320,640]{1,0:T(8,128)(2,1)S(1)} %get-tuple-element.21), channel_id=1, source_target_pairs={{0,1},{1,0},{2,3},{3,2},{4,5},{5,4},{6,7},{7,6},{8,9},{9,8},{10,11... | collective-permute-start | bytes 1228808 | tf_op jit(solution)/shard_map/ppermute | solution.py:73
  11.2 86.7 %collective-permute-start = (bf16[1024,640]{1,0:T(8,128)(2,1)}, bf16[1024,640]{1,0:T(8,128)(2,1)}, u32[]{:S(2)}, u32[]{:S(2)}) collective-permute-start(bf16[1024,640]{1,0:T(8,128)(2,1)} %param.14), channel_id=1, source_target_pairs={{0,1},{1,0},{2,3},{3,2},{4,5},{5,4},{6,7},{7,6},{8,9},{9,8},{10,11... | collective-permute-start | bytes 3932168 | tf_op jit(solution)/shard_map/ppermute | solution.py:79
  13.3 9.9 %copy-start.17 = (s32[1,32]{1,0:T(1,128)S(1)}, s32[1,32]{1,0:T(1,128)}, u32[]{:S(2)}) copy-start(s32[1,32]{1,0:T(1,128)} %param.21) | copy-start | bytes 388
  13.3 10.3 %copy-start.3 = (bf16[1,64,7168]{2,1,0:T(8,128)(2,1)S(1)}, bf16[1,64,7168]{2,1,0:T(8,128)(2,1)}, u32[]{:S(2)}) copy-start(bf16[1,64,7168]{2,1,0:T(8,128)(2,1)} %param.18) | copy-start | bytes 2752516
  14.4 67.9 %all-to-all-start = ((bf16[8,1,64,640]{3,2,1,0:T(8,128)(2,1)}), bf16[8,1,64,640]{3,2,1,0:T(8,128)(2,1)S(1)}, u32[]{:S(2)}, u32[]{:S(2)}) async-start(bf16[8,1,64,640]{3,2,1,0:T(8,128)(2,1)} %copy.20), calls=%async_computation | async-start | bytes 1310720 | tf_op jit(solution)/shard_map/all_to_all | solution.py:92
  19.3 34.1 %collective-permute-start.3 = (bf16[1,5120,64]{1,2,0:T(8,128)(2,1)S(1)}, bf16[1,5120,64]{1,2,0:T(8,128)(2,1)}, u32[]{:S(2)}, u32[]{:S(2)}) collective-permute-start(bf16[1,5120,64]{1,2,0:T(8,128)(2,1)S(1)} %copy-done.9), channel_id=1, source_target_pairs={{0,8},{8,0},{1,9},{9,1},{2,10},{10,2},{3,11},{11,3},{4,12},{12,4},... | collective-permute-start | bytes 1966088 | tf_op jit(solution)/shard_map/ppermute | solution.py:96
  53.4 42.7 %collective-permute-start.2 = (bf16[320,640]{1,0:T(8,128)(2,1)}, bf16[320,640]{1,0:T(8,128)(2,1)}, u32[]{:S(2)}, u32[]{:S(2)}) collective-permute-start(bf16[320,640]{1,0:T(8,128)(2,1)} %collective-permute-done.1), channel_id=1, source_target_pairs={{0,8},{8,0},{1,9},{9,1},{2,10},{10,2},{3,11},{11,3},{4,12},{12,4},... | collective-permute-start | bytes 1228808 | tf_op jit(solution)/shard_map/ppermute | solution.py:74
  82.3 95.3 %all-to-all-start.1 = ((bf16[8,1,64,1536]{3,2,1,0:T(8,128)(2,1)}), bf16[8,1,64,1536]{3,2,1,0:T(8,128)(2,1)S(1)}, u32[]{:S(2)}, u32[]{:S(2)}) async-start(bf16[8,1,64,1536]{3,2,1,0:T(8,128)(2,1)} %copy.21), calls=%async_computation.1 | async-start | bytes 3145728 | tf_op jit(solution)/shard_map/all_to_all | solution.py:92
  88.4 11.1 %collective-permute-start.4 = (bf16[8,64,640]{2,1,0:T(8,128)(2,1)S(1)}, bf16[8,64,640]{2,1,0:T(8,128)(2,1)S(1)}, u32[]{:S(2)}, u32[]{:S(2)}) collective-permute-start(bf16[8,64,640]{2,1,0:T(8,128)(2,1)S(1)} %bitcast.74), channel_id=1, source_target_pairs={{0,8},{8,0},{1,9},{9,1},{2,10},{10,2},{3,11},{11,3},{4,12},{12,4},... | collective-permute-start | bytes 1966088 | tf_op jit(solution)/shard_map/ppermute | solution.py:94
  88.4 9.6 %copy-start.10 = (bf16[1024,1280]{1,0:T(8,128)(2,1)S(1)}, bf16[1024,1280]{1,0:T(8,128)(2,1)}, u32[]{:S(2)}) copy-start(bf16[1024,1280]{1,0:T(8,128)(2,1)} %constant_dynamic-update-slice_fusion.1) | copy-start | bytes 7864324
  97.4 54.2 %collective-permute-start.10 = (bf16[320,1920]{1,0:T(8,128)(2,1)}, bf16[320,1920]{1,0:T(8,128)(2,1)S(1)}, u32[]{:S(2)}, u32[]{:S(2)}) collective-permute-start(bf16[320,1920]{1,0:T(8,128)(2,1)} %collective-permute-done.9), channel_id=1, source_target_pairs={{0,8},{8,0},{1,9},{9,1},{2,10},{10,2},{3,11},{11,3},{4,12},{12,4},... | collective-permute-start | bytes 3686408 | tf_op jit(solution)/shard_map/ppermute | solution.py:74
  99.5 69.6 %copy-start.11 = (bf16[1024,1280]{1,0:T(8,128)(2,1)}, bf16[1024,1280]{1,0:T(8,128)(2,1)S(1)}, u32[]{:S(2)}) copy-start(bf16[1024,1280]{1,0:T(8,128)(2,1)S(1)} %constant_dynamic-update-slice_fusion) | copy-start | bytes 7864324
  99.7 20.4 %slice-start = ((s8[10485760]{0:T(1024)(128)(4,1)}), s8[4194304]{0:T(1024)(128)(4,1)S(1)}, s32[]{:S(2)}) async-start(s8[10485760]{0:T(1024)(128)(4,1)} %bitcast.70), calls=%async_computation.2 | async-start | bytes 8388608
  99.7 20.4 %slice-start.1 = ((s8[10485760]{0:T(1024)(128)(4,1)}), s8[4194304]{0:T(1024)(128)(4,1)S(1)}, s32[]{:S(2)}) async-start(s8[10485760]{0:T(1024)(128)(4,1)} %bitcast.70), calls=%async_computation.3 | async-start | bytes 8388608
  104.2 13.2 %collective-permute-start.5 = (bf16[1024,128]{0,1:T(8,128)(2,1)S(1)}, bf16[1024,128]{0,1:T(8,128)(2,1)S(1)}, u32[]{:S(2)}, u32[]{:S(2)}) collective-permute-start(bf16[1024,128]{0,1:T(8,128)(2,1)S(1)} %fusion.34), channel_id=1, source_target_pairs={{0,1},{1,0},{2,3},{3,2},{4,5},{5,4},{6,7},{7,6},{8,9},{9,8},{10,11... | collective-permute-start | bytes 786440 | tf_op jit(solution)/shard_map/ppermute | solution.py:137
  106.2 13.8 %slice-start.2 = ((s8[10485760]{0:T(1024)(128)(4,1)}), s8[2097152]{0:T(1024)(128)(4,1)S(1)}, s32[]{:S(2)}) async-start(s8[10485760]{0:T(1024)(128)(4,1)} %bitcast.70), calls=%async_computation.4 | async-start | bytes 4194304
  108.4 60.7 %copy-start.2 = (f32[1024,640]{1,0:T(8,128)}, f32[1024,640]{1,0:T(8,128)S(1)}, u32[]{:S(2)}) copy-start(f32[1024,640]{1,0:T(8,128)S(1)} %get-tuple-element.37) | copy-start | bytes 7864324
  108.5 60.6 %collective-permute-start.11 = (bf16[1024,640]{1,0:T(8,128)(2,1)S(1)}, bf16[1024,640]{1,0:T(8,128)(2,1)S(1)}, u32[]{:S(2)}, u32[]{:S(2)}) collective-permute-start(bf16[1024,640]{1,0:T(8,128)(2,1)S(1)} %get-tuple-element.11), channel_id=1, source_target_pairs={{0,2},{1,3},{8,10},{9,11},{16,18},{17,19},{24,26},{25,27}} | collective-permute-start | bytes 3932168 | tf_op jit(solution)/shard_map/ppermute | solution.py:167
  111.9 57.2 %collective-permute-start.14 = (bf16[1024,640]{1,0:T(8,128)(2,1)S(1)}, bf16[1024,640]{1,0:T(8,128)(2,1)S(1)}, u32[]{:S(2)}, u32[]{:S(2)}) collective-permute-start(bf16[1024,640]{1,0:T(8,128)(2,1)S(1)} %get-tuple-element.11), channel_id=1, source_target_pairs={{6,4},{7,5},{14,12},{15,13},{22,20},{23,21},{30,28},{31,29}} | collective-permute-start | bytes 3932168 | tf_op jit(solution)/shard_map/ppermute | solution.py:168
  117.4 29.4 %collective-permute-start.6 = (bf16[1024,128]{0,1:T(8,128)(2,1)S(1)}, bf16[1024,128]{0,1:T(8,128)(2,1)S(1)}, u32[]{:S(2)}, u32[]{:S(2)}) collective-permute-start(bf16[1024,128]{0,1:T(8,128)(2,1)S(1)} %fusion.37), channel_id=1, source_target_pairs={{0,2},{1,3},{2,0},{3,1},{4,6},{5,7},{6,4},{7,5},{8,10},{9,11},{10,... | collective-permute-start | bytes 786440 | tf_op jit(solution)/shard_map/ppermute | solution.py:137
  146.9 15.1 %collective-permute-start.7 = (bf16[1024,128]{0,1:T(8,128)(2,1)S(1)}, bf16[1024,128]{0,1:T(8,128)(2,1)S(1)}, u32[]{:S(2)}, u32[]{:S(2)}) collective-permute-start(bf16[1024,128]{0,1:T(8,128)(2,1)S(1)} %fusion.35), channel_id=1, source_target_pairs={{0,4},{1,5},{2,6},{3,7},{4,0},{5,1},{6,2},{7,3},{8,12},{9,13},{10,... | collective-permute-start | bytes 786440 | tf_op jit(solution)/shard_map/ppermute | solution.py:137
  162.3 6.8 %copy-start.5 = (bf16[640,640]{1,0:T(8,128)(2,1)S(1)}, bf16[640,640]{1,0:T(8,128)(2,1)}, u32[]{:S(2)}) copy-start(bf16[640,640]{1,0:T(8,128)(2,1)} %get-tuple-element.17) | copy-start | bytes 2457604
  163.1 10.8 %copy-start.15 = (bf16[1024,1024]{0,1:T(8,128)(2,1)}, bf16[1024,1024]{0,1:T(8,128)(2,1)S(1)}, u32[]{:S(2)}) copy-start(bf16[1024,1024]{0,1:T(8,128)(2,1)S(1)} %get-tuple-element.30) | copy-start | bytes 6291460
  173.8 29.6 %collective-permute-start.12 = (bf16[1024,640]{1,0:T(8,128)(2,1)}, bf16[1024,640]{1,0:T(8,128)(2,1)S(1)}, u32[]{:S(2)}, u32[]{:S(2)}) collective-permute-start(bf16[1024,640]{1,0:T(8,128)(2,1)} %get-tuple-element.22), channel_id=1, source_target_pairs={{0,2},{1,3},{2,4},{3,5},{8,10},{9,11},{10,12},{11,13},{16,18},{17,... | collective-permute-start | bytes 3932168 | tf_op jit(solution)/shard_map/ppermute | solution.py:167
  175.2 28.2 %collective-permute-start.15 = (bf16[1024,640]{1,0:T(8,128)(2,1)}, bf16[1024,640]{1,0:T(8,128)(2,1)}, u32[]{:S(2)}, u32[]{:S(2)}) collective-permute-start(bf16[1024,640]{1,0:T(8,128)(2,1)} %get-tuple-element.23), channel_id=1, source_target_pairs={{4,2},{5,3},{6,4},{7,5},{12,10},{13,11},{14,12},{15,13},{20,18},{2... | collective-permute-start | bytes 3932168 | tf_op jit(solution)/shard_map/ppermute | solution.py:168
  177.6 38.6 %collective-permute-start.8 = (bf16[8,64,1536]{2,1,0:T(8,128)(2,1)S(1)}, bf16[8,64,1536]{2,1,0:T(8,128)(2,1)S(1)}, u32[]{:S(2)}, u32[]{:S(2)}) collective-permute-start(bf16[8,64,1536]{2,1,0:T(8,128)(2,1)S(1)} %bitcast.67), channel_id=1, source_target_pairs={{0,8},{8,0},{1,9},{9,1},{2,10},{10,2},{3,11},{11,3},{4,12},{12,4},... | collective-permute-start | bytes 4718600 | tf_op jit(solution)/shard_map/ppermute | solution.py:94
  208.0 33.0 %collective-permute-start.13 = (bf16[1024,640]{1,0:T(8,128)(2,1)S(1)}, bf16[1024,640]{1,0:T(8,128)(2,1)S(1)}, u32[]{:S(2)}, u32[]{:S(2)}) collective-permute-start(bf16[1024,640]{1,0:T(8,128)(2,1)S(1)} %get-tuple-element.12), channel_id=1, source_target_pairs={{0,2},{1,3},{2,4},{3,5},{4,6},{5,7},{8,10},{9,11},{10,12},{11,13},... | collective-permute-start | bytes 3932168 | tf_op jit(solution)/shard_map/ppermute | solution.py:167
  214.6 30.7 %collective-permute-start.16 = (bf16[1024,640]{1,0:T(8,128)(2,1)S(1)}, bf16[1024,640]{1,0:T(8,128)(2,1)S(1)}, u32[]{:S(2)}, u32[]{:S(2)}) collective-permute-start(bf16[1024,640]{1,0:T(8,128)(2,1)S(1)} %get-tuple-element.13), channel_id=1, source_target_pairs={{2,0},{3,1},{4,2},{5,3},{6,4},{7,5},{10,8},{11,9},{12,10},{13,11},... | collective-permute-start | bytes 3932168 | tf_op jit(solution)/shard_map/ppermute | solution.py:168
  222.9 23.9 %copy-start.1 = (s32[2,6]{1,0:T(2,128)S(1)}, s32[2,6]{1,0:T(2,128)}, u32[]{:S(2)}) copy-start(s32[2,6]{1,0:T(2,128)} %param.23) | copy-start | bytes 148
  (11 other events, 26.7 us)

commit v3 on v1

--- a/solution.py
+++ b/solution.py
@@ -1,7 +1,371 @@
+import functools
+
 import jax
 import jax.numpy as jnp
 from jax import lax
+from jax.experimental import pallas as pl
+from jax.experimental.pallas import tpu as pltpu
 from jax.sharding import PartitionSpec as P
+
+MESH = pl.DeviceIdType.MESH
+
+
+def project(
+    tensor_size,
+    hidden_hbm,
+    w_qkv_hbm,
+    context,
+    w_out,
+    maps,
+    a_own,
+    store_row,
+    base_qkv,
+    base_out,
+    got,
+    low,
+    hidden,
+    w_qkv,
+    context_two,
+    w_two,
+    going,
+    above,
+    below,
+    a_two,
+    low_part,
+    low_in,
+    load_sem,
+    pair_send,
+    pair_recv,
+    w_send,
+    w_recv,
+    line_send,
+    up_recv,
+    down_recv,
+    maps_send,
+    maps_recv,
+    core_send,
+    core_recv,
+    hand_send,
+    hand_recv,
+    a_send,
+    a_recv,
+    low_send,
+    low_recv,
+    share_send,
+    share_recv,
+):
+    f32, bf16 = jnp.float32, jnp.bfloat16
+    group, core, t = lax.axis_index("groups"), lax.axis_index("dp"), lax.axis_index("tensor")
+    depth = tensor_size // 2
+    z, y = t // 2, t % 2
+    rows, part = context.shape
+    last = depth - 1
+
+    def device(core_of, tensor_of):
+        return (group, core_of, tensor_of)
+
+    pair = device(core, 2 * z + 1 - y)
+    twin = device(1 - core, t)
+    peers = [lax.rem(t + i, tensor_size) for i in range(1, tensor_size)]
+
+    loads = [
+        pltpu.make_async_copy(w_qkv_hbm, w_qkv, load_sem.at[0]),
+        pltpu.make_async_copy(hidden_hbm, hidden, load_sem.at[1]),
+    ]
+    for load in loads:
+        load.start()
+
+    barrier = pltpu.get_barrier_semaphore()
+    for peer in peers:
+        pl.semaphore_signal(barrier, inc=1, device_id=device(core, peer), device_id_type=MESH)
+    pl.semaphore_signal(barrier, inc=1, device_id=twin, device_id_type=MESH)
+    pl.semaphore_wait(barrier, tensor_size)
+
+    def remote(src, dst, send, recv, to):
+        return pltpu.make_async_remote_copy(
+            src_ref=src, dst_ref=dst, send_sem=send, recv_sem=recv, device_id=to, device_id_type=MESH
+        )
+
+    half_rows = rows // 2
+    halves = [pl.ds(h * half_rows, half_rows) for h in range(2)]
+
+    def trade(h):
+        return remote(context.at[halves[h]], context_two.at[halves[h]], pair_send.at[h], pair_recv.at[h], pair)
+
+    core_rows = pl.ds(pl.multiple_of(core * (part // 2), 16), part // 2)
+
+    def weights(d):
+        their_cols = pl.ds(pl.multiple_of((2 * d + 1 - y) * part, 128), part)
+        return remote(w_out.at[core_rows, their_cols], w_two.at[d, core_rows], w_send.at[d], w_recv.at[d], pair)
+
+    def hand(d):
+        return remote(w_two.at[d, core_rows], w_two.at[d, core_rows], hand_send.at[d], hand_recv.at[d], twin)
+
+    def hand_on(d, up, s):
+        weights(d).wait_recv()
+        hand(d).start()
+
+    rank = maps.shape[0] // tensor_size
+
+    def map_rows(source):
+        return pl.ds(pl.multiple_of(source * rank, 16), rank)
+
+    def map_copy(i):
+        src, dst = maps.at[map_rows(peers[i])], got.at[0, map_rows(t)]
+        return remote(src, dst, maps_send.at[i], maps_recv.at[i], device(core, peers[i]))
+
+    def pass_on(i):
+        source = lax.rem(t + tensor_size - 1 - i, tensor_size)
+        src, dst = got.at[0, map_rows(source)], got.at[1, map_rows(source)]
+        return remote(src, dst, core_send.at[i], core_recv.at[i], twin)
+
+    a_copy = remote(a_own, a_two.at[pl.ds(rank, rank)], a_send, a_recv, twin)
+    share_rows = rows // tensor_size
+
+    def rows_of(device_index):
+        return pl.ds(pl.multiple_of(device_index * share_rows, 16), share_rows)
+
+    def low_copy(i):
+        to = device(core, peers[i])
+        return remote(low_part.at[rows_of(peers[i])], low_in.at[i], low_send.at[i], low_recv.at[i], to)
+
+    def share(i):
+        to = device(core, peers[i])
+        return remote(low.at[rows_of(t)], low.at[rows_of(t)], share_send.at[i], share_recv.at[i], to)
+
+    def each(s, act):
+        if s == last:
+            act(z, None, s)
+            return
+
+        @pl.when(z <= s)
+        def _():
+            act(z + last - s, True, s)
+
+        @pl.when(z >= last - s)
+        def _():
+            act(z - last + s, False, s)
+
+    def chunk(d, tile):
+        cols = pl.ds(pl.multiple_of((2 * d + y) * part, 128), part)
+        own = jnp.dot(context[tile, :], w_out[:, cols], preferred_element_type=f32)
+        return own + jnp.dot(context_two[tile, :], w_two[d], preferred_element_type=f32)
+
+    def line_copy(d, up, s, h):
+        slot = above if up else below
+        recv = up_recv if up else down_recv
+        to = device(core, lax.rem(t + (2 if up else tensor_size - 2), tensor_size))
+        src, dst = going.at[d, halves[h]], slot.at[s, halves[h]]
+        return remote(src, dst, line_send.at[d, h], recv.at[s, h], to)
+
+    tile_rows = min(half_rows, 256)
+    tiles = rows // tile_rows
+    half_tiles = half_rows // tile_rows
+
+    def tile_of(i):
+        return pl.ds(pl.multiple_of(i * tile_rows, tile_rows), tile_rows)
+
+    def over(count, start, body):
+        def step(i, carry):
+            body(tile_of(start + i))
+            return carry
+
+        lax.fori_loop(0, count, step, 0)
+
+    def send(d, up, s, h):
+        if h == 0:
+            hand(d).wait_recv()
+
+        def first(tile):
+            base_out[tile, :] = chunk(d, tile)
+
+        def plain(tile):
+            going[d, tile, :] = base_out[tile, :].astype(bf16)
+
+        def added(tile):
+            came = (above if up else below)[s - 1, tile, :].astype(f32)
+            going[d, tile, :] = (base_out[tile, :] + came).astype(bf16)
+
+        over(half_tiles, h * half_tiles, first)
+        if s == 0:
+            over(half_tiles, h * half_tiles, plain)
+        else:
+            inner = z > 0 if up else z < last
+
+            @pl.when(inner)
+            def _():
+                line_copy(d, up, s - 1, h).wait_recv()
+                over(half_tiles, h * half_tiles, added)
+
+            @pl.when(jnp.logical_not(inner))
+            def _():
+                over(half_tiles, h * half_tiles, plain)
+
+        line_copy(d, up, s, h).start()
+
+    each(0, lambda d, up, s: weights(d).start())
+    trade(0).start()
+    for i in range(tensor_size - 1):
+        map_copy(i).start()
+    own_maps = remote(
+        maps.at[map_rows(t)],
+        got.at[1, map_rows(t)],
+        core_send.at[tensor_size - 1],
+        core_recv.at[tensor_size - 1],
+        twin,
+    )
+    own_maps.start()
+    a_copy.start()
+    got[0, map_rows(t)] = maps[map_rows(t)]
+    a_two[:rank] = a_own[...]
+    each(0, hand_on)
+    trade(0).wait_recv()
+    trade(1).start()
+    each(0, functools.partial(send, h=0))
+    trade(1).wait_recv()
+    each(1, lambda d, up, s: weights(d).start())
+    each(0, functools.partial(send, h=1))
+
+    for load in loads:
+        load.wait()
+    a_copy.wait()
+    lanes = lax.broadcasted_iota(jnp.int32, (tile_rows, 2 * rank), 1)
+    own_id = jnp.where(lanes < rank, core, 1 - core) * tensor_size + t
+
+    def joined(tile):
+        base_qkv[tile, :] = jnp.dot(hidden[tile, :], w_qkv[...], preferred_element_type=f32)
+        down = lax.dot_general(
+            hidden[tile, :], a_two[...], (((1,), (1,)), ((), ())), preferred_element_type=f32
+        )
+        down = jnp.where(store_row[tile, :] == own_id, down, 0.0)
+        low_part[tile, :] = down + pltpu.roll(down, rank, 1)
+
+    def low_out(tile):
+        total = jnp.zeros((tile_rows, 2 * rank), f32)
+        for c in range(2):
+            down = lax.dot_general(
+                context[tile, :], got[c, :, :part], (((1,), (1,)), ((), ())), preferred_element_type=f32
+            )
+            first = (core if c == 0 else 1 - core) * tensor_size
+            for j in range(tensor_size // 2):
+                ids = first + 2 * j + jnp.where(lanes < rank, 0, 1)
+                cut = down[:, 2 * rank * j : 2 * rank * (j + 1)]
+                total = total + jnp.where(store_row[tile, :] == ids, cut, 0.0)
+        total = total + pltpu.roll(total, rank, 1)
+        low_part[tile, :] = jnp.where(lanes < rank, low_part[tile, :], total)
+
+    over(tiles, 0, joined)
+    for s in range(1, last):
+        each(s, hand_on)
+        each(s + 1, lambda d, up, s: weights(d).start())
+        for h in range(2):
+            each(s, functools.partial(send, h=h))
+        if s == 1:
+            for i in range(tensor_size - 1):
+                map_copy(i).wait_recv()
+                pass_on(i).start()
+    each(last, hand_on)
+
+    for i in range(tensor_size - 1):
+        pass_on(i).wait()
+        map_copy(i).wait_send()
+    own_maps.wait()
+    over(tiles, 0, low_out)
+    for i in range(tensor_size - 1):
+        low_copy(i).start()
+    hand(z).wait_recv()
+
+    def own(tile):
+        base_out[tile, :] = chunk(z, tile)
+
+    over(tiles, 0, own)
+    whole = low_part[rows_of(t)]
+    for i in range(tensor_size - 1):
+        low_copy(i).wait_recv()
+        whole = whole + low_in[i]
+    low[rows_of(t)] = whole.astype(bf16)
+    for i in range(tensor_size - 1):
+        share(i).start()
+
+    for h in range(2):
+        for up in (True, False):
+
+            @pl.when(z > 0 if up else z < last)
+            def _():
+                line_copy(z, up, last - 1, h).wait_recv()
+
+                def added(tile):
+                    came = (above if up else below)[last - 1, tile, :].astype(f32)
+                    base_out[tile, :] = base_out[tile, :] + came
+
+                over(half_tiles, h * half_tiles, added)
+
+    for i in range(tensor_size - 1):
+        share(i).wait()
+        low_copy(i).wait_send()
+    for s in range(depth):
+        each(s, lambda d, up, s: (weights(d).wait_send(), hand(d).wait_send()))
+    for h in range(2):
+        trade(h).wait_send()
+        for s in range(last):
+            each(s, lambda d, up, s: line_copy(d, up, s, h).wait_send())
+
+
+def projections(tensor_size, hidden, w_qkv, context, w_out, maps, a_own, store_row):
+    f32, bf16 = jnp.float32, jnp.bfloat16
+    rows, part = context.shape
+    depth, rank = tensor_size // 2, a_own.shape[0]
+    in_vmem = pl.BlockSpec(memory_space=pltpu.VMEM)
+    in_hbm = pl.BlockSpec(memory_space=pl.ANY)
+    dma = pltpu.SemaphoreType.DMA
+    return pl.pallas_call(
+        functools.partial(project, tensor_size),
+        out_shape=(
+            jax.ShapeDtypeStruct((rows, w_qkv.shape[1]), f32),
+            jax.ShapeDtypeStruct((rows, part), f32),
+            jax.ShapeDtypeStruct((2,) + maps.shape, bf16),
+            jax.ShapeDtypeStruct((rows, 2 * rank), bf16),
+        ),
+        in_specs=[in_hbm, in_hbm] + [in_vmem] * 5,
+        out_specs=(in_vmem,) * 4,
+        scratch_shapes=[
+            pltpu.VMEM(hidden.shape, bf16),
+            pltpu.VMEM(w_qkv.shape, bf16),
+            pltpu.VMEM(context.shape, bf16),
+            pltpu.VMEM((depth, part, part), bf16),
+            pltpu.VMEM((depth, rows, part), bf16),
+            pltpu.VMEM((depth - 1, rows, part), bf16),
+            pltpu.VMEM((depth - 1, rows, part), bf16),
+            pltpu.VMEM((2 * rank, hidden.shape[1]), bf16),
+            pltpu.VMEM((rows, 2 * rank), f32),
+            pltpu.VMEM((tensor_size - 1, rows // tensor_size, 2 * rank), f32),
+            dma((2,)),
+            dma((2,)),
+            dma((2,)),
+            dma((depth,)),
+            dma((depth,)),
+            dma((depth, 2)),
+            dma((depth - 1, 2)),
+            dma((depth - 1, 2)),
+            dma((tensor_size - 1,)),
+            dma((tensor_size - 1,)),
+            dma((tensor_size,)),
+            dma((tensor_size,)),
+            dma((depth,)),
+            dma((depth,)),
+            dma(()),
+            dma(()),
+        ]
+        + [dma((tensor_size - 1,))] * 4,
+        compiler_params=pltpu.CompilerParams(
+            collective_id=0, has_side_effects=True, vmem_limit_bytes=62 * 1024 * 1024
+        ),
+        cost_estimate=pl.CostEstimate(
+            flops=2 * rows * (hidden.shape[1] * w_qkv.shape[1] + 2 * part * part * depth),
+            bytes_accessed=2 * (hidden.size + w_qkv.size + w_out.size + context.size),
+            transcendentals=0,
+        ),
+    )(hidden, w_qkv, context, w_out, maps, a_own, store_row)
 
 
 def chunk_order(depth):
@@ -27,7 +391,7 @@
     return jnp.sum(jnp.where(inside, seg_row[None, :], 0), axis=1)
 
 
-def shards(
+def plain_shards(
     hidden,
     context,
     w_qkv,
@@ -140,6 +504,80 @@
     return (qkv, attn_out)
 
 
+def shards(
+    hidden,
+    context,
+    w_qkv,
+    w_out,
+    a_qkv,
+    b_qkv,
+    a_out,
+    b_out,
+    seg_len,
+    seg_use,
+    used_list,
+    adapter_slot,
+):
+    f32, bf16 = jnp.float32, jnp.bfloat16
+    tensor_size = lax.axis_size("tensor")
+    dp_size = lax.axis_size("dp")
+    t = lax.axis_index("tensor")
+    dp_rank = lax.axis_index("dp")
+    tok_rows, model_width = hidden.shape
+    owned, _, rank = a_qkv.shape
+    out_part = model_width // tensor_size
+    qkv_part = b_qkv.shape[2] // tensor_size
+    if tensor_size % 2 or tensor_size < 6 or out_part % 128 or qkv_part % 128 or owned != 1 or rank != 64 or tok_rows % 512:
+        return plain_shards(
+            hidden, context, w_qkv, w_out, a_qkv, b_qkv, a_out, b_out,
+            seg_len, seg_use, used_list, adapter_slot,
+        )
+
+    used = used_list[dp_rank][:, None] == jnp.arange(adapter_slot.shape[0], dtype=jnp.int32)[None, :]
+    row_of_use = jnp.sum(jnp.where(used, adapter_slot[None, :], 0), axis=1)
+    store_row = token_rows(seg_len[0], seg_use[0], row_of_use, tok_rows)
+
+    def split(maps, part):
+        return jnp.transpose(maps.reshape(rank, tensor_size, part), (1, 0, 2))
+
+    sent = jnp.concatenate(
+        (
+            split(jnp.transpose(a_out, (0, 2, 1)), out_part),
+            split(b_out, out_part),
+            split(b_qkv, qkv_part),
+        ),
+        axis=2,
+    )
+    sent = sent.reshape(-1, sent.shape[2])
+    store_lanes = jnp.broadcast_to(store_row[:, None], (tok_rows, 2 * rank))
+    base_qkv, base_out, got, low = projections(
+        tensor_size, hidden, w_qkv, context, w_out, sent, jnp.transpose(a_qkv[0]), store_lanes
+    )
+    got = got.reshape(-1, got.shape[2])
+    up_out = got[:, out_part : 2 * out_part]
+    up_qkv = got[:, 2 * out_part :]
+
+    half = tensor_size * owned
+    first, second = dp_rank * half, (1 - dp_rank) * half
+
+    def lane_mask(rows):
+        return store_row[:, None] == jnp.repeat(rows, rank)[None, :]
+
+    rows = jnp.arange(half, dtype=jnp.int32)
+    row_mask = lane_mask(jnp.concatenate((first + rows, second + rows)))
+
+    def expand(start, maps):
+        lanes = jnp.arange(row_mask.shape[1], dtype=jnp.int32) % rank + start
+        copies = (jnp.arange(2 * rank, dtype=jnp.int32)[:, None] == lanes[None, :]).astype(bf16)
+        spread = jnp.dot(low, copies, preferred_element_type=f32).astype(bf16)
+        spread = jnp.where(row_mask, spread, jnp.zeros((), bf16))
+        return jnp.dot(spread, maps, preferred_element_type=f32)
+
+    qkv = (base_qkv + expand(0, up_qkv)).astype(bf16)
+    attn_out = (base_out + expand(rank, up_out)).astype(bf16)
+    return (qkv, attn_out)
+
+
 def solution(mesh):
     placed = (
         P(("groups", "dp"), None),

time: 225 us -> 192 us (0.85)
  Pallas kernels: 0 us -> 169 us
  matrix products: 70.3 us -> 11.9 us
  blocking collectives: 52.7 us -> 0 us
  waiting for transfers between devices: 41.6 us -> 0 us
  starting transfers between devices: 30.6 us -> 0 us
  other arithmetic: 15.7 us -> 4.82 us
  between operations: 7.32 us -> 0.73 us
    pallas_call x0 -> x1, Pallas kernels: none -> 169 us  [projections(): pl.pallas_call(functools.partial(project, tensor_size), out_shape=(jax.Sh...]
    dot_general x13 -> x2, matrix products: 70.3 us -> 11.9 us  [expand(): return jnp.dot(spread, maps, preferred_element_type=f32)]
    psum x1 -> x0, blocking collectives: 52.7 us -> none  [shards(): lax.psum((pick(low_a, own_mask), pick(low_b, row_mask)), 'tensor')]
    ppermute x12 -> x0, waiting for transfers between devices: 31.3 us -> none  [the longest x4 27.6 us: shards(): mine = lax.ppermute(partial(order[k], 1 - y).astype(bf16), 'tensor', swap)]
    ppermute x12 -> x0, starting transfers between devices: 25.3 us -> none  [the longest x3 13.7 us: shards(): up = lax.ppermute(outgoing_up.astype(bf16), 'tensor', up_pairs)]
    convert_element_type x2 -> x0, other arithmetic: 11.6 us -> none  [shards(): up = lax.ppermute(outgoing_up.astype(bf16), 'tensor', up_pairs)]
    all_to_all x1 -> x0, waiting for transfers between devices: 10.3 us -> none  [shards(): lax.all_to_all(sent, 'tensor', split_axis=0, concat_axis=0, tiled=True)]
    all_to_all x1 -> x0, starting transfers between devices: 5.29 us -> none  [shards(): lax.all_to_all(sent, 'tensor', split_axis=0, concat_axis=0, tiled=True)]
  transfers between devices with their start and end apart: 13 -> 0, of which waited for: 4 -> 0; matrix products, arithmetic and copies ran while one was open for 32% -> 0% of each run, Pallas kernels for 0% -> 0%
where the time goes in v3:
time: 192 us; the launch traced here: 191 us
  Pallas kernels  169 us (88%)
  matrix products  11.9 us (6%)
  other arithmetic  4.82 us (3%)
  local copies, waits for them, and re-layouts  4.71 us (2%)
    pallas_call x1, Pallas kernels, projections(): pl.pallas_call(functools.partial(project, tensor_size), out_shape=(jax.Sh...  169 us
    dot_general x2, matrix products, expand(): return jnp.dot(spread, maps, preferred_element_type=f32)  11.9 us

profile of v3, /device:TPU:0, one launch (start us, length us, event | category | flops | bytes accessed | tf_op | source)
XLA Modules:
  0.0 191.5 jit_solution(15138898082032016112)
XLA Ops:
  0.6 0.0 copy-start
  0.6 0.7 copy-done
  1.3 0.8 select_reduce_fusion.3
  2.2 0.7 select_reduce_fusion.2
  2.9 0.8 select_reduce_fusion.1
  3.7 0.7 fusion.26
  4.3 0.1 select_reduce_fusion
  4.4 1.0 broadcast_in_dim.89.store_row
  5.4 0.0 copy-start.1
  5.4 1.2 copy.20
  6.7 1.2 copy.21
  7.9 0.2 copy_bitcast_fusion.1
  8.1 0.0 copy-done.1
  8.1 0.1 copy.22
  8.2 0.1 copy.26
  8.4 1.6 pad_maximum_fusion
  10.0 169.3 %shard_map.131 = (f32[1024,896]{1,0:T(8,128)}, f32[1024,640]{1,0:T(8,128)}, bf16[2,512,2176]{2,1,0:T(8,128)(2,1)}, bf16[1024,128]{1,0:T(8,128)(2,1)}) custom-call(bf16[1024,5120]{1,0:T(8,128)(2,1)} %hidden_hbm.1, bf16[5120,896]{1,0:T(8,128)(2,1)} %w_qkv_hbm.1, bf16[1024,640]{1,0:T(8,128)(2,1)} %context.1, bf16[640,5120]{1,0:T(8,128)(2,1)} %w_out.1, ...), custom_call_target="tpu_custom_call" | custom-call | flops 16106127360 | bytes 27525120 | tf_op jit(solution)/shard_map/pallas_call | solution.py:321
  179.4 0.1 pad_add_fusion
  179.4 0.1 broadcast_in_dim.90
  179.5 0.1 eq.83
  179.6 0.0 copy-start.2
  179.6 5.7 %add_convert_fusion.1 = bf16[1024,640]{1,0:T(8,128)(2,1)} fusion(f32[1024,640]{1,0:T(8,128)} %get-tuple-element.9, bf16[1024,128]{1,0:T(8,128)(2,1)} %get-tuple-element.7, s32[1024]{0:T(1024)S(1)} %eq.83, s32[1024]{0:T(1024)S(1)} %select_reduce_fusion, bf16[1024,2176]{1,0:T(8,128)(2,1)} %bitcast.45, s32[1024]{0:T(1024)S(1)} %broadcast_add_fusion), kind=kOutput, calls=%fused_computation.3 | convolution fusion | flops 1615200256 | bytes 5517312 | tf_op jit(solution)/shard_map/dot_general | solution.py:574
  185.3 0.0 copy-done.2
  185.3 6.1 %add_convert_fusion = bf16[1024,896]{1,0:T(8,128)(2,1)} fusion(f32[1024,896]{1,0:T(8,128)} %get-tuple-element.6, bf16[1024,2176]{1,0:T(8,128)(2,1)} %bitcast.46, bf16[1024,128]{1,0:T(8,128)(2,1)S(1)} %copy-done.2, s32[1024]{0:T(1024)S(1)} %eq.83, s32[1024]{0:T(1024)S(1)} %select_reduce_fusion, s32[1024]{0:T(1024)S(1)} %add_select_fusion), kind=kOutput, calls=%fused_computation.2 | convolution fusion | flops 2152595456 | bytes 7614464 | tf_op jit(solution)/shard_map/dot_general | solution.py:574
  (4 shorter events, 0.0 us)
Async XLA Ops:
  0.6 0.7 copy-start
  5.4 2.6 %copy-start.1 = (bf16[1,64,7168]{2,1,0:T(8,128)(2,1)S(1)}, bf16[1,64,7168]{2,1,0:T(8,128)(2,1)}, u32[]{:S(2)}) copy-start(bf16[1,64,7168]{2,1,0:T(8,128)(2,1)} %param.17) | copy-start | bytes 2752516
  179.6 5.7 %copy-start.2 = (bf16[1024,128]{1,0:T(8,128)(2,1)S(1)}, bf16[1024,128]{1,0:T(8,128)(2,1)}, u32[]{:S(2)}) copy-start(bf16[1024,128]{1,0:T(8,128)(2,1)} %get-tuple-element.7) | copy-start | bytes 786436

commit v4 on v3

--- a/solution.py
+++ b/solution.py
@@ -223,7 +223,8 @@
     trade(1).start()
     each(0, functools.partial(send, h=0))
     trade(1).wait_recv()
-    each(1, lambda d, up, s: weights(d).start())
+    for s in range(1, depth):
+        each(s, lambda d, up, s: weights(d).start())
     each(0, functools.partial(send, h=1))
 
     for load in loads:
@@ -255,16 +256,15 @@
         low_part[tile, :] = jnp.where(lanes < rank, low_part[tile, :], total)
 
     over(tiles, 0, joined)
+    for s in range(1, depth):
+        each(s, hand_on)
     for s in range(1, last):
-        each(s, hand_on)
-        each(s + 1, lambda d, up, s: weights(d).start())
         for h in range(2):
             each(s, functools.partial(send, h=h))
         if s == 1:
             for i in range(tensor_size - 1):
                 map_copy(i).wait_recv()
                 pass_on(i).start()
-    each(last, hand_on)
 
     for i in range(tensor_size - 1):
         pass_on(i).wait()

time: 192 us -> 205 us (1.068)
  Pallas kernels: 169 us -> 182 us
    pallas_call x1, Pallas kernels: 169 us -> 182 us  [projections(): pl.pallas_call(functools.partial(project, tensor_size), out_shape=(jax.Sh...]
where the time goes in v4:
time: 205 us; the launch traced here: 204 us
  Pallas kernels  182 us (89%)
  matrix products  11.9 us (6%)
  other arithmetic  4.82 us (2%)
  local copies, waits for them, and re-layouts  4.71 us (2%)
    pallas_call x1, Pallas kernels, projections(): pl.pallas_call(functools.partial(project, tensor_size), out_shape=(jax.Sh...  182 us
    dot_general x2, matrix products, expand(): return jnp.dot(spread, maps, preferred_element_type=f32)  11.9 us

profile of v4, /device:TPU:0, one launch (start us, length us, event | category | flops | bytes accessed | tf_op | source)
XLA Modules:
  0.0 204.5 jit_solution(15874181919225058351)
XLA Ops:
  0.6 0.0 copy-start
  0.6 0.7 copy-done
  1.3 0.8 select_reduce_fusion.3
  2.2 0.7 select_reduce_fusion.2
  2.9 0.8 select_reduce_fusion.1
  3.7 0.7 fusion.26
  4.3 0.1 select_reduce_fusion
  4.4 1.0 broadcast_in_dim.89.store_row
  5.4 0.0 copy-start.1
  5.4 1.2 copy.20
  6.7 1.2 copy.21
  7.9 0.2 copy_bitcast_fusion.1
  8.1 0.0 copy-done.1
  8.1 0.1 copy.22
  8.2 0.1 copy.26
  8.4 1.6 pad_maximum_fusion
  10.0 182.4 %shard_map.131 = (f32[1024,896]{1,0:T(8,128)}, f32[1024,640]{1,0:T(8,128)}, bf16[2,512,2176]{2,1,0:T(8,128)(2,1)}, bf16[1024,128]{1,0:T(8,128)(2,1)}) custom-call(bf16[1024,5120]{1,0:T(8,128)(2,1)} %hidden_hbm.1, bf16[5120,896]{1,0:T(8,128)(2,1)} %w_qkv_hbm.1, bf16[1024,640]{1,0:T(8,128)(2,1)} %context.1, bf16[640,5120]{1,0:T(8,128)(2,1)} %w_out.1, ...), custom_call_target="tpu_custom_call" | custom-call | flops 16106127360 | bytes 27525120 | tf_op jit(solution)/shard_map/pallas_call | solution.py:321
  192.4 0.1 pad_add_fusion
  192.5 0.1 broadcast_in_dim.90
  192.5 0.1 eq.83
  192.6 0.0 copy-start.2
  192.6 5.7 %add_convert_fusion.1 = bf16[1024,640]{1,0:T(8,128)(2,1)} fusion(f32[1024,640]{1,0:T(8,128)} %get-tuple-element.9, bf16[1024,128]{1,0:T(8,128)(2,1)} %get-tuple-element.7, s32[1024]{0:T(1024)S(1)} %eq.83, s32[1024]{0:T(1024)S(1)} %select_reduce_fusion, bf16[1024,2176]{1,0:T(8,128)(2,1)} %bitcast.45, s32[1024]{0:T(1024)S(1)} %broadcast_add_fusion), kind=kOutput, calls=%fused_computation.3 | convolution fusion | flops 1615200256 | bytes 5517312 | tf_op jit(solution)/shard_map/dot_general | solution.py:574
  198.3 0.0 copy-done.2
  198.3 6.2 %add_convert_fusion = bf16[1024,896]{1,0:T(8,128)(2,1)} fusion(f32[1024,896]{1,0:T(8,128)} %get-tuple-element.6, bf16[1024,2176]{1,0:T(8,128)(2,1)} %bitcast.46, bf16[1024,128]{1,0:T(8,128)(2,1)S(1)} %copy-done.2, s32[1024]{0:T(1024)S(1)} %eq.83, s32[1024]{0:T(1024)S(1)} %select_reduce_fusion, s32[1024]{0:T(1024)S(1)} %add_select_fusion), kind=kOutput, calls=%fused_computation.2 | convolution fusion | flops 2152595456 | bytes 7614464 | tf_op jit(solution)/shard_map/dot_general | solution.py:574
  (4 shorter events, 0.0 us)
Async XLA Ops:
  0.6 0.7 copy-start
  5.4 2.6 %copy-start.1 = (bf16[1,64,7168]{2,1,0:T(8,128)(2,1)S(1)}, bf16[1,64,7168]{2,1,0:T(8,128)(2,1)}, u32[]{:S(2)}) copy-start(bf16[1,64,7168]{2,1,0:T(8,128)(2,1)} %param.17) | copy-start | bytes 2752516
  192.6 5.7 %copy-start.2 = (bf16[1024,128]{1,0:T(8,128)(2,1)S(1)}, bf16[1024,128]{1,0:T(8,128)(2,1)}, u32[]{:S(2)}) copy-start(bf16[1024,128]{1,0:T(8,128)(2,1)} %get-tuple-element.7) | copy-start | bytes 786436
